TPU v7x, 256 devices: a whole 4x4x8 slice. The times are simulated.
256 devices in a mesh: dp: 8 (over y, core), shard: 32 (over x, z).
Axes of the slice: x: 4, y: 4, z: 8, core: 2. Of those that a mesh axis runs over, the one named last changes fastest.
Arguments:
- grads: bfloat16 [8, 36, 1024, 1024], P('dp', None, 'shard'), may hold values from -0.59765625 to 0.59765625
- vec_grads: bfloat16 [8, 32, 1024], P('dp', 'shard'), may hold values from -0.59765625 to 0.59765625
- factor_left: float32 [96, 1024, 1024], P('shard', 'dp'), may hold values from -6 to 6
- factor_right: float32 [96, 1024, 1024], P('shard', None, 'dp'), may hold values from -6 to 6
- root_left: bfloat16 [96, 1024, 1024], P('shard', None, 'dp'), may hold values from -0.1875 to 0.1875
- root_right: bfloat16 [96, 1024, 1024], P('shard', None, 'dp'), may hold values from -0.1875 to 0.1875
- vec_param: float32 [32, 1024], P('shard', 'dp'), may hold values from -10 to 10
- vec_first: float32 [32, 1024], P('shard', 'dp'), may hold values from -0.6 to 0.6
- vec_second: float32 [32, 1024], P('shard', 'dp'), may hold values from 0.001 to 0.1
- bucket_block: int32 [36], replicated, may hold values from 0 to 35, each once
- block_slot: int32 [36], replicated, may hold values from 0 to 95, as said below
- decay_mask: int32 [32, 1024], P('shard', 'dp'), may hold values 0 or 1
Outputs:
- block_update: bfloat16 [36, 1024, 1024], P(None, 'shard')
- new_left: float32 [96, 1024, 1024], P('shard', 'dp')
- new_right: float32 [96, 1024, 1024], P('shard', None, 'dp')
- vec_update: bfloat16 [32, 1024], P('shard')
- new_first: float32 [32, 1024], P('shard', 'dp')
- new_second: float32 [32, 1024], P('shard', 'dp')
Inputs may be any that keep to these rules, and one draw needn't show every extreme that they name: `bucket_block`: a permutation of the block numbers. `block_slot`: distinct values; a value's owner is value // 3 and its place there value % 3; no owner holds more than 3 blocks and some owner holds exactly 3.
All inputs are finite; a program needn't handle non-finite values. No bound on the sum of `decay_mask` on one device may be relied on, other than what follows from the above.
Results may differ from a plain program's by a relative error of at most 0.022.
Values may be sent and summed in bfloat16 or wider, within the bound.
No kernel may reach another device: no remote copies, remote signals or barrier semaphores. Data moves between devices by JAX's collectives and lax.ppermute only.
A program may use at most 128 MiB of HBM per device.

v0:
```python
import jax
import jax.numpy as jnp
from jax import lax
from jax.experimental import pallas as pl
from jax.experimental.pallas import tpu as pltpu
from jax.sharding import Mesh
from jax.sharding import PartitionSpec as P

BETA_STAT = 0.95
ADAM_ONE = 0.9
ADAM_TWO = 0.95
ADAM_EPS = 1e-08
DECAY = 0.1

RING = 4
CORES = 2
OWNERS = 32
SLOTS = 3
NBLK = 36
PER = NBLK // RING
BLOCK = 1024
ROWS = BLOCK // OWNERS
TILE = 128
PASS = 512
HALF = BLOCK // CORES
BODY = PER * ROWS
HEAD = (PER + 1) // 2
A_ROWS = HEAD * ROWS
B_ROWS = BODY - A_ROWS
BS_ROWS = B_ROWS + 16
SHARE = 2 * BLOCK + 32
FULL = NBLK * ROWS
BF16 = jnp.bfloat16
F32 = jnp.float32
T_OWNER = 40
T_SEL = 80
T_REL = 84
TABLE = 88
VMEM_LIMIT = 24 * 1024 * 1024


def whole():
    return pl.BlockSpec(memory_space=pltpu.VMEM)


def call(
    body, grid, in_specs, out_specs, out_shape, scratch=(), flops=0, moved=0, limit=VMEM_LIMIT
):
    return pl.pallas_call(
        body,
        name=body.__name__,
        grid_spec=pltpu.PrefetchScalarGridSpec(
            num_scalar_prefetch=2,
            grid=grid,
            in_specs=in_specs,
            out_specs=out_specs,
            scratch_shapes=list(scratch),
        ),
        out_shape=out_shape,
        compiler_params=pltpu.CompilerParams(vmem_limit_bytes=limit),
        cost_estimate=pl.CostEstimate(flops=flops, bytes_accessed=moved, transcendentals=0),
    )


def outside():
    return pl.BlockSpec(memory_space=pltpu.HBM)


def stay(x):
    return jax.tree.map(lambda a: pltpu.with_memory_space_constraint(a, pltpu.HBM), x)


def tile_at(index):
    return pl.ds(pl.multiple_of(index * TILE, TILE), TILE)


def rows_at(index, size=ROWS):
    return pl.ds(pl.multiple_of(index * size, size), size)


def dot(a, b):
    return jnp.dot(a, b, preferred_element_type=F32)


def front_body(pos, spare, maps, grad, vec, tab, own, own_vec, seat, ranks, sems):
    copies = [
        pltpu.make_async_copy(grad.at[:, tile_at(2 * j + pos[1])], own.at[j], sems.at[j])
        for j in range(RING)
    ]
    copies.append(pltpu.make_async_copy(vec, own_vec, sems.at[RING]))
    for copy in copies:
        copy.start()
    for s in range(OWNERS * SLOTS):
        seat[s] = -1
    for p in range(NBLK):
        seat[maps[NBLK + maps[p]]] = p
    for k in range(RING):
        tab[T_SEL + k] = 0
    rank = jnp.int32(0)
    for s in range(OWNERS * SLOTS):
        p = seat[s]
        tab[rank] = p
        tab[T_OWNER + rank] = s // SLOTS
        ranks[s] = rank
        rank = rank + jnp.where(p >= 0, 1, 0)
    for k in range(SLOTS):
        s = pos[2] * SLOTS + k
        held = seat[s] >= 0
        plane = lax.rem(ranks[s], RING)
        tab[T_REL + k] = jnp.where(held, lax.bitwise_xor(pos[0], plane), -1)
        ahead = T_SEL + lax.bitwise_xor(pos[0], plane)
        tab[ahead] = jnp.where(held, k, tab[ahead])
    for copy in copies:
        copy.wait()


def front(pos, maps, grad, vec):
    smem = pl.BlockSpec(memory_space=pltpu.SMEM)
    return call(
        front_body,
        (),
        [smem, outside(), outside()],
        [smem, whole(), whole()],
        [
            jax.ShapeDtypeStruct((TABLE,), jnp.int32),
            jax.ShapeDtypeStruct((RING, FULL, TILE), BF16),
            jax.ShapeDtypeStruct((1, 1, BLOCK), BF16),
        ],
        scratch=[
            pltpu.SMEM((OWNERS * SLOTS,), jnp.int32),
            pltpu.SMEM((OWNERS * SLOTS,), jnp.int32),
            pltpu.SemaphoreType.DMA((RING + 1,)),
        ],
        moved=4 * FULL * HALF,
    )(pos, pos, maps, stay(grad), stay(vec))


def pair_body(pos, tab, own, got, vec, got_vec, give_a, keep_a, give_b, keep_b):
    lanes_of = [tile_at(2 * j + pos[1]) for j in range(RING)]
    first = {0: (keep_a, 0), 3: (keep_a, 1), 1: (give_a, 0), 2: (give_a, 1)}
    second = {0: (keep_b, 0), 1: (keep_b, 1), 3: (give_b, 0), 2: (give_b, 1)}
    for k in range(RING):
        plane = lax.bitwise_xor(pos[0], k)
        for i in range(PER):
            at = rows_at(tab[RING * i + plane])
            out, part = first[k] if i < HEAD else second[k]
            low = part * A_ROWS + ROWS * i if i < HEAD else part * BS_ROWS + ROWS * (i - HEAD)
            for j, lanes in enumerate(lanes_of):
                here = slice(TILE * j, TILE * (j + 1))
                out[low : low + ROWS, here] = own[j, at, :] + got[at, lanes]
    for j, lanes in enumerate(lanes_of):
        both = vec[0, :, lanes].astype(F32) + got_vec[0, :, lanes].astype(F32)
        strip = jnp.broadcast_to(both, (16, TILE)).astype(BF16)
        for out, part in second.values():
            low = part * BS_ROWS + B_ROWS
            out[low : low + 16, TILE * j : TILE * (j + 1)] = strip


def pair(pos, tab, own, got, vec, got_vec):
    return call(
        pair_body,
        (),
        [whole()] * 4,
        [whole()] * 4,
        [jax.ShapeDtypeStruct((2 * n, HALF), BF16) for n in (A_ROWS, A_ROWS, BS_ROWS, BS_ROWS)],
        moved=6 * FULL * HALF,
    )(pos, tab, own, got, vec, got_vec)


def total_body(
    pos, tab, a0, a1, a2, b0, b1, b2, param, first, second, mask, send, new_first, new_second, step
):
    send[...] = jnp.zeros(send.shape, BF16)
    for i in range(PER):
        refs, low = ((a0, a1, a2), ROWS * i) if i < HEAD else ((b0, b1, b2), ROWS * (i - HEAD))
        parts = [ref[low : low + ROWS, :].astype(F32) for ref in refs]
        total = (parts[0] + parts[1]) + parts[2]
        send[rows_at(tab[T_OWNER + RING * i + pos[0]]), :] = total.astype(BF16)
    strips = [ref[B_ROWS:BS_ROWS, tile_at(pos[0])].astype(F32) for ref in (b0, b1, b2)]
    vec_sum = ((strips[0] + strips[1]) + strips[2])[0:1]
    one = ADAM_ONE * first[...] + (1.0 - ADAM_ONE) * vec_sum
    two = ADAM_TWO * second[...] + (1.0 - ADAM_TWO) * vec_sum * vec_sum
    new_first[...] = one
    new_second[...] = two
    update = one / (jnp.sqrt(two) + ADAM_EPS) + DECAY * mask[...].astype(F32) * param[...]
    step[...] = jnp.broadcast_to(update, (16, TILE)).astype(BF16)


def total(pos, tab, parts, param, first, second, mask):
    return call(
        total_body,
        (),
        [whole()] * 10,
        [whole()] * 4,
        [
            pltpu.HBM((BLOCK, HALF), BF16),
            jax.ShapeDtypeStruct((1, TILE), F32),
            jax.ShapeDtypeStruct((1, TILE), F32),
            jax.ShapeDtypeStruct((16, TILE), BF16),
        ],
        moved=12 * BODY * HALF + 2 * BLOCK * HALF,
    )(pos, tab, *parts, param, first, second, mask)


def roots_body(pos, tab, left, right, *outs):
    for k in range(RING):
        slot = tab[T_SEL + k]
        outs[k][0:BLOCK, :] = left[slot]
        for j in range(RING):
            for n, tile in enumerate((2 * j + pos[1], 2 * j + 1 - pos[1])):
                at = BLOCK + HALF * n + TILE * j
                outs[k][at : at + TILE, :] = right[slot, rows_at(tile, TILE), :]


def roots(pos, tab, left, right):
    return call(
        roots_body,
        (),
        [whole()] * 2,
        [whole()] * RING,
        [pltpu.HBM((2 * BLOCK, TILE), BF16)] * RING,
        moved=4 * (SLOTS + RING) * BLOCK * TILE,
    )(pos, tab, left, right)


def update_body(pos, tab, mine, other, right, *refs):
    ours, theirs = refs[:RING], refs[RING : 2 * RING]
    out, left, applied, result, sems, out_sems = refs[2 * RING :]
    core = pos[1]
    copies = []
    for k in range(RING):
        plane = lax.bitwise_xor(pos[0], k)
        for n, (ref, tile) in enumerate(((ours[k], 2 * plane + core), (theirs[k], 2 * plane + 1 - core))):
            copies.append(
                pltpu.make_async_copy(ref.at[0:BLOCK, :], left.at[:, tile_at(tile)], sems.at[n, k])
            )
    for copy in copies:
        copy.start()
    applied[...] = (
        dot(mine[...], right[0:HALF, :]) + dot(other[...], right[HALF:BLOCK, :])
    ).astype(BF16)
    for copy in copies:
        copy.wait()
    stores = []
    for n in range(BLOCK // PASS):
        at = slice(PASS * n, PASS * (n + 1))
        result[at, :] = dot(left[at, :], applied[...]).astype(BF16)
        stores.append(pltpu.make_async_copy(result.at[at, :], out.at[at, :], out_sems.at[n]))
        stores[n].start()
    for copy in stores:
        copy.wait()


def update(pos, tab, mine, other, right, ours, theirs):
    return call(
        update_body,
        (),
        [whole()] * 3 + [outside()] * (2 * RING),
        outside(),
        pltpu.HBM((BLOCK, HALF), BF16),
        scratch=[
            pltpu.VMEM((BLOCK, BLOCK), BF16),
            pltpu.VMEM((BLOCK, HALF), BF16),
            pltpu.VMEM((BLOCK, HALF), BF16),
            pltpu.SemaphoreType.DMA((2, RING)),
            pltpu.SemaphoreType.DMA((BLOCK // PASS,)),
        ],
        flops=4 * BLOCK * BLOCK * HALF,
        moved=16 * BLOCK * HALF,
    )(pos, tab, mine, other, right, *stay(ours), *theirs)


def turn(core, buf, turned, some):
    for j in range(RING):
        at = slice(TILE * j, TILE * (j + 1))
        turned[at, :] = buf[:, at].T
        some[at, :] = buf[rows_at(2 * j + core, TILE), :]


def gram_first_body(pos, tab, mine, r0, r1, r2, r3, across, down, right, turned, some, sems):
    copies = []
    for k, ref in enumerate((r0, r1, r2, r3)):
        lanes = tile_at(lax.bitwise_xor(pos[0], k))
        copies.append(
            pltpu.make_async_copy(ref.at[BLOCK : 2 * BLOCK, :], right.at[:, lanes], sems.at[k])
        )
        copies[k].start()
    turn(pos[1], mine, turned, some)
    across[...] = dot(some[...], turned[...])
    down[...] = dot(turned[...], mine[...]).astype(BF16)
    for copy in copies:
        copy.wait()


def gram_first(pos, tab, mine, sides):
    return call(
        gram_first_body,
        (),
        [whole()] + [outside()] * RING,
        [whole()] * 3,
        [
            jax.ShapeDtypeStruct((HALF, BLOCK), F32),
            jax.ShapeDtypeStruct((HALF, HALF), BF16),
            jax.ShapeDtypeStruct((BLOCK, HALF), BF16),
        ],
        scratch=[
            pltpu.VMEM((HALF, BLOCK), BF16),
            pltpu.VMEM((HALF, HALF), BF16),
            pltpu.SemaphoreType.DMA((RING,)),
        ],
        flops=2 * BLOCK * BLOCK * HALF,
        moved=4 * BLOCK * BLOCK,
    )(pos, tab, mine, *stay(sides))


def gram_body(
    pos, tab, mine, other, half, down, step, step_other, o0, o1, o2, o3, turned, some, across, down_other, held, sems
):
    core = pos[1]
    outs = (o0, o1, o2, o3)
    copies = []

    def send(k, n, low, high):
        copy = pltpu.make_async_copy(
            held.at[k, low:high, :], outs[k].at[low:high, :], sems.at[k, n]
        )
        copy.start()
        copies.append(copy)

    turn(core, other, turned, some)
    across[...] = (half[...] + dot(some[...], turned[...])).astype(BF16)
    for k in range(RING):
        plane = lax.bitwise_xor(pos[0], k)
        for t in range(BLOCK // TILE):
            at = slice(TILE * t, TILE * (t + 1))
            held[k, at, :] = across[rows_at(plane, TILE), at]
        send(k, 0, 0, BLOCK)
    down_other[...] = dot(turned[...], mine[...]).astype(BF16)
    for k in range(RING):
        plane = lax.bitwise_xor(pos[0], k)
        for j in range(RING):
            at = slice(TILE * j, TILE * (j + 1))
            lanes = tile_at(plane)
            held[k, rows_at(BLOCK // TILE + 2 * j + core, TILE), :] = down[at, lanes]
            held[k, rows_at(BLOCK // TILE + 2 * j + 1 - core, TILE), :] = down_other[at, lanes]
        held[k, 2 * BLOCK : 2 * BLOCK + 16, :] = step[...]
        held[k, 2 * BLOCK + 16 : SHARE, :] = step_other[...]
        send(k, 1, BLOCK, SHARE)
    for copy in copies:
        copy.wait()


def gram(pos, tab, mine, other, half, down, step, step_other):
    return call(
        gram_body,
        (),
        [whole()] * 6,
        [outside()] * RING,
        [pltpu.HBM((SHARE, TILE), BF16)] * RING,
        scratch=[
            pltpu.VMEM((HALF, BLOCK), BF16),
            pltpu.VMEM((HALF, HALF), BF16),
            pltpu.VMEM((HALF, BLOCK), BF16),
            pltpu.VMEM((HALF, HALF), BF16),
            pltpu.VMEM((RING, SHARE, TILE), BF16),
            pltpu.SemaphoreType.DMA((RING, 2)),
        ],
        flops=2 * BLOCK * BLOCK * HALF,
        moved=8 * BLOCK * HALF,
    )(pos, tab, mine, other, half, down, step, step_other)


def stats_body(
    pos, tab, left, right, g0, g1, g2, g3, new_left, new_right, vec, rows, cols, held, sems, gram_sems
):
    gets = [pltpu.make_async_copy(g, held.at[k], gram_sems.at[k]) for k, g in enumerate((g0, g1, g2, g3))]
    loads, stores = [], []
    for s in range(SLOTS):
        pairs = ((left, rows, new_left), (right, cols, new_right))
        loads += [
            pltpu.make_async_copy(a.at[s], b.at[s], sems.at[0, s, n])
            for n, (a, b, c) in enumerate(pairs)
        ]
        stores += [
            pltpu.make_async_copy(b.at[s], c.at[s], sems.at[1, s, n])
            for n, (a, b, c) in enumerate(pairs)
        ]
    for copy in gets + loads:
        copy.start()
    for k in range(RING):
        gets[k].wait()
        plane = lax.bitwise_xor(pos[0], k)
        vec[:, tile_at(2 * plane + pos[1])] = held[k, 2 * BLOCK : 2 * BLOCK + 16, :]
        vec[:, tile_at(2 * plane + 1 - pos[1])] = held[k, 2 * BLOCK + 16 : SHARE, :]
    for s in range(SLOTS):
        source = tab[T_REL + s]
        some = source >= 0
        k = jnp.maximum(source, 0)
        loads[2 * s].wait()
        for t in range(BLOCK // TILE):
            at = slice(TILE * t, TILE * (t + 1))
            add = jnp.where(some, held[k, at, :].astype(F32), 0.0)
            rows[s, :, at] = BETA_STAT * rows[s, :, at] + (1.0 - BETA_STAT) * add
        stores[2 * s].start()
        loads[2 * s + 1].wait()
        add = jnp.where(some, held[k, BLOCK : 2 * BLOCK, :].astype(F32), 0.0)
        cols[s] = BETA_STAT * cols[s] + (1.0 - BETA_STAT) * add
        stores[2 * s + 1].start()
    for copy in stores:
        copy.wait()


def stats(pos, tab, left, right, grams):
    return call(
        stats_body,
        (),
        [outside()] * (2 + RING),
        [outside(), outside(), whole()],
        [
            jax.ShapeDtypeStruct((SLOTS, TILE, BLOCK), F32),
            jax.ShapeDtypeStruct((SLOTS, BLOCK, TILE), F32),
            jax.ShapeDtypeStruct((16, BLOCK), BF16),
        ],
        scratch=[
            pltpu.VMEM((SLOTS, TILE, BLOCK), F32),
            pltpu.VMEM((SLOTS, BLOCK, TILE), F32),
            pltpu.VMEM((RING, SHARE, TILE), BF16),
            pltpu.SemaphoreType.DMA((2, SLOTS, 2)),
            pltpu.SemaphoreType.DMA((RING,)),
        ],
        moved=16 * SLOTS * BLOCK * TILE + 16 * BLOCK * TILE,
    )(pos, tab, *stay([left, right, *grams]))


def back_body(pos, tab, got, out):
    for i in range(PER):
        at = rows_at(tab[T_OWNER + RING * i + pos[0]])
        out[ROWS * i : ROWS * (i + 1), :] = got[at, :]


def back(pos, tab, got):
    return call(
        back_body,
        (),
        [whole()],
        whole(),
        jax.ShapeDtypeStruct((BODY, HALF), BF16),
        moved=2 * (BLOCK + BODY) * HALF,
    )(pos, tab, got)


def place_body(parts, pos, tab, *refs):
    out, rows, sems = refs[-3:]
    core = pos[1]
    copies = []
    for n, (k, first, count) in enumerate(parts):
        plane = lax.bitwise_xor(pos[0], k)
        ours, theirs = refs[2 * n], refs[2 * n + 1]
        for i in range(count):
            at = slice(ROWS * i, ROWS * (i + 1))
            slab = len(copies)
            here = slice(ROWS * slab, ROWS * (slab + 1))
            for j in range(RING):
                lanes = slice(TILE * j, TILE * (j + 1))
                rows[here, tile_at(2 * j + core)] = ours[at, lanes]
                rows[here, tile_at(2 * j + 1 - core)] = theirs[at, lanes]
            target = out.at[rows_at(tab[RING * (first + i) + plane]), :]
            copies.append(pltpu.make_async_copy(rows.at[here, :], target, sems.at[slab]))
            copies[-1].start()
    for copy in copies:
        copy.wait()


def place(pos, tab, parts, arrays, onto=None):
    def place_part(*refs):
        place_body(parts, *refs)

    slabs = sum(count for _, _, count in parts)
    extra = () if onto is None else (onto,)
    return pl.pallas_call(
        place_part,
        name="place_part",
        grid_spec=pltpu.PrefetchScalarGridSpec(
            num_scalar_prefetch=2,
            grid=(),
            in_specs=[whole()] * (2 * len(parts)) + [outside()] * len(extra),
            out_specs=outside(),
            scratch_shapes=[
                pltpu.VMEM((ROWS * slabs, BLOCK), BF16),
                pltpu.SemaphoreType.DMA((slabs,)),
            ],
        ),
        out_shape=jax.ShapeDtypeStruct((FULL, BLOCK), BF16),
        input_output_aliases={} if onto is None else {2 + 2 * len(parts): 0},
        compiler_params=pltpu.CompilerParams(vmem_limit_bytes=VMEM_LIMIT),
        cost_estimate=pl.CostEstimate(
            flops=0, bytes_accessed=4 * ROWS * slabs * BLOCK, transcendentals=0
        ),
    )(pos, tab, *arrays, *extra)


def hop(x, k):
    return lax.ppermute(x, "y", [(i, i ^ k) for i in range(RING)])


def spread(x):
    far, near, other = lax.optimization_barrier((hop(x[2], 2), x[1], x[3]))
    return [x[0], hop(near, 1), far, hop(other, 3)]


def swap(x):
    return lax.ppermute(x, "core", [(0, 1), (1, 0)])


def route(x):
    x = x.reshape(OWNERS, ROWS, HALF)
    return lax.all_to_all(x, ("x", "z"), 0, 0).reshape(BLOCK, HALF)


def shards(
    grads,
    vec_grads,
    factor_left,
    factor_right,
    root_left,
    root_right,
    vec_param,
    vec_first,
    vec_second,
    bucket_block,
    block_slot,
    decay_mask,
):
    y, core = lax.axis_index("y"), lax.axis_index("core")
    owner = lax.axis_index(("x", "z"))
    pos = jnp.stack([y, core, owner]).astype(jnp.int32)
    grad = grads.reshape(FULL, BLOCK)
    got, got_vec = swap(grad), swap(vec_grads)
    tab, own, vec = front(pos, jnp.concatenate([bucket_block, block_slot]), grad, vec_grads)
    give_a, keep_a, give_b, keep_b = pair(pos, tab, own, got, vec, got_vec)
    got_a, got_b = hop(give_a, 1), hop(give_b, 3)
    last_a = hop(keep_a[A_ROWS:] + got_a[A_ROWS:], 3)
    last_b = hop(keep_b[BS_ROWS:] + got_b[BS_ROWS:], 1)
    parts = [keep_a, got_a, last_a, keep_b, got_b, last_b]
    sides = roots(pos, tab, root_left, root_right)
    parts, sides = lax.optimization_barrier((parts, sides))
    send, new_first, new_second, step = total(
        pos, tab, parts, vec_param, vec_first, vec_second, decay_mask
    )
    send, sides = lax.optimization_barrier((send, sides))
    sides = spread(sides)
    mine = route(send)
    step_other = swap(step)
    mine, sides, step_other = lax.optimization_barrier((mine, sides, step_other))
    other = swap(mine)
    across, down, right = gram_first(pos, tab, mine, sides)
    other, sides, across, down, right = lax.optimization_barrier(
        (other, sides, across, down, right)
    )
    grams = gram(pos, tab, mine, other, across, down, step, step_other)
    others = [swap(x) for x in sides]
    others, grams = lax.optimization_barrier((others, grams))
    result = update(pos, tab, mine, other, right, sides, others)
    result, grams = lax.optimization_barrier((result, grams))
    near, other_near, far = hop(grams[1], 1), hop(grams[3], 3), hop(grams[2], 2)
    got = route(result)
    got, near, other_near, far = lax.optimization_barrier((got, near, other_near, far))
    grams = [grams[0], near, far, other_near]
    piece = back(pos, tab, got)
    near, near_other = hop(piece, 3), hop(piece, 1)
    new_left, new_right, vec_update = stats(pos, tab, factor_left, factor_right, grams)
    near, near_other, new_left, new_right, vec_update = lax.optimization_barrier(
        (near, near_other, new_left, new_right, vec_update[0:1])
    )
    far = [hop(near[:A_ROWS], 1), hop(near_other[A_ROWS:], 3)]
    both = []
    for x in (piece, near, near_other):
        both += [x, swap(x)]
    placed = place(pos, tab, ((0, 0, PER), (3, 0, PER), (1, 0, PER)), both)
    far, placed = lax.optimization_barrier((far, placed))
    both = [far[0], swap(far[0]), far[1], swap(far[1])]
    block_update = place(pos, tab, ((2, 0, HEAD), (2, HEAD, PER - HEAD)), both, placed)
    return (
        block_update.reshape(NBLK, ROWS, BLOCK),
        new_left,
        new_right,
        vec_update,
        new_first,
        new_second,
    )


def solution(mesh):
    fine = Mesh(mesh.devices.reshape(RING, CORES, 4, 8), ("y", "core", "x", "z"))
    dp, shard = ("y", "core"), ("x", "z")
    return jax.shard_map(
        shards,
        mesh=fine,
        in_specs=(
            P(dp, None, shard, None),
            P(dp, shard, None),
            P(shard, dp, None),
            P(shard, None, dp),
            P(shard, None, dp),
            P(shard, None, dp),
            P(shard, dp),
            P(shard, dp),
            P(shard, dp),
            P(),
            P(),
            P(shard, dp),
        ),
        out_specs=(
            P(None, shard, None),
            P(shard, dp, None),
            P(shard, None, dp),
            P(shard, None),
            P(shard, dp),
            P(shard, dp),
        ),
        check_vma=False,
    )
```

profile of v0, /device:TPU:1, one launch (start us, length us, event | category | flops | bytes accessed | tf_op | source)
XLA Modules:
  0.0 135.8 jit_solution(14202168625706255491)
XLA Ops:
  0.6 3.3 %collective-permute-start = (bf16[1152,1024]{1,0:T(8,128)(2,1)}, bf16[1152,1024]{1,0:T(8,128)(2,1)S(1)}, u32[]{:S(2)}, u32[]{:S(2)}) collective-permute-start(bf16[1152,1024]{1,0:T(8,128)(2,1)} %bitcast.16), channel_id=1, source_target_pairs={{0,32},{32,0},{1,33},{33,1},{2,34},{34,2},{3,35},{35,3},{4,36},{36... | collective-permute-start | bytes 7077896 | tf_op jit(solution)/shard_map/ppermute | solution.py:512
  4.9 3.3 %front_body.1 = (s32[88]{0:T(128)S(1)}, bf16[4,1152,128]{2,1,0:T(8,128)(2,1)S(1)}, bf16[1,1,1024]{2,1,0:T(2,128)(2,1)S(1)}) custom-call(s32[3]{0:T(128)S(1)} %pad_add_fusion.pos.spare.refs_0_, s32[3]{0:T(128)S(1)} %pad_add_fusion.pos.spare.refs_0_, s32[72]{0:T(128)S(1)} %pad_add_fusion.1.maps, bf16[1152,1024]{1,0:T(8,128)(2,1)} %bitcast.17, ...), custom_call_target="tpu_custom_call" | custom-call | bytes 2359296 | tf_op jit(solution)/shard_map/front_body/pallas_call | solution.py:119
  9.5 1.4 %collective-permute-start.4 = (bf16[288,512]{1,0:T(8,128)(2,1)S(1)}, bf16[288,512]{1,0:T(8,128)(2,1)S(1)}, u32[]{:S(2)}, u32[]{:S(2)}) collective-permute-start(bf16[288,512]{1,0:T(8,128)(2,1)S(1)} %get-tuple-element.94), channel_id=1, source_target_pairs={{0,192},{64,128},{128,64},{192,0},{1,193},{65,129},{129,65},{193,1... | collective-permute-start | bytes 884744 | tf_op jit(solution)/shard_map/ppermute | solution.py:503
  10.9 7.5 %collective-permute-done.2.a1 = bf16[320,512]{1,0:T(8,128)(2,1)S(1)} collective-permute-done((bf16[320,512]{1,0:T(8,128)(2,1)S(1)}, bf16[320,512]{1,0:T(8,128)(2,1)S(1)}, u32[]{:S(2)}, u32[]{:S(2)}) %collective-permute-start.2) | collective-permute-done | bytes 327712 | tf_op jit(solution)/shard_map/ppermute | solution.py:503
  19.6 2.0 %roots_body.1 = (bf16[2048,128]{1,0:T(8,128)(2,1)}, bf16[2048,128]{1,0:T(8,128)(2,1)}, bf16[2048,128]{1,0:T(8,128)(2,1)}, bf16[2048,128]{1,0:T(8,128)(2,1)}) custom-call(s32[3]{0:T(128)S(1)} %pad_add_fusion.pos.spare.refs_0_, s32[88]{0:T(128)S(1)} %get-tuple-element.88.tab.refs_1_, bf16[3,1024,128]{2,1,0:T(8,128)(2,1)S(1)} %copy-done, ...), custom_call_target="tpu_custom_call" | custom-call | bytes 3670016 | tf_op jit(solution)/shard_map/roots_body/pallas_call | solution.py:216
  21.6 2.0 %collective-permute-done.5.b2 = bf16[144,512]{1,0:T(8,128)(2,1)S(1)} collective-permute-done((bf16[144,512]{1,0:T(8,128)(2,1)S(1)}, bf16[144,512]{1,0:T(8,128)(2,1)S(1)}, u32[]{:S(2)}, u32[]{:S(2)}) %collective-permute-start.5) | collective-permute-done | bytes 147488 | tf_op jit(solution)/shard_map/ppermute | solution.py:503
  24.2 1.7 %total_body.1 = (bf16[1024,512]{1,0:T(8,128)(2,1)}, f32[1,128]{1,0:T(1,128)}, f32[1,128]{1,0:T(1,128)}, bf16[16,128]{1,0:T(8,128)(2,1)S(1)}) custom-call(s32[3]{0:T(128)S(1)} %pad_add_fusion.pos.spare.refs_0_, s32[88]{0:T(128)S(1)} %get-tuple-element.88.tab.refs_1_, bf16[320,512]{1,0:T(8,128)(2,1)S(1)} %get-tuple-element.99.a0, ...), custom_call_target="tpu_custom_call" | custom-call | bytes 2818048 | tf_op jit(solution)/shard_map/total_body/pallas_call | solution.py:190
  25.9 10.7 %all-to-all-start = ((bf16[32,32,512]{2,1,0:T(8,128)(2,1)}), bf16[32,32,512]{2,1,0:T(8,128)(2,1)S(1)}, u32[]{:S(2)}, u32[]{:S(2)}) async-start(bf16[32,32,512]{2,1,0:T(8,128)(2,1)} %bitcast.18), calls=%async_computation | async-start | bytes 2097152 | tf_op jit(solution)/shard_map/all_to_all | solution.py:517
  37.1 12.0 %collective-permute-done.6.r2.refs_2_ = bf16[2048,128]{1,0:T(8,128)(2,1)S(1)} collective-permute-done((bf16[2048,128]{1,0:T(8,128)(2,1)S(1)}, bf16[2048,128]{1,0:T(8,128)(2,1)S(1)}, u32[]{:S(2)}, u32[]{:S(2)}) %collective-permute-start.6) | collective-permute-done | bytes 524320 | tf_op jit(solution)/shard_map/ppermute | solution.py:503
  49.2 1.4 %collective-permute-start.8 = (bf16[2048,128]{1,0:T(8,128)(2,1)}, bf16[2048,128]{1,0:T(8,128)(2,1)S(1)}, u32[]{:S(2)}, u32[]{:S(2)}) collective-permute-start(bf16[2048,128]{1,0:T(8,128)(2,1)} %get-tuple-element.117), channel_id=1, source_target_pairs={{0,192},{64,128},{128,64},{192,0},{1,193},{65,129},{129,65},{193,1... | collective-permute-start | bytes 1572872 | tf_op jit(solution)/shard_map/ppermute | solution.py:503
  50.6 3.6 %collective-permute-start.9 = (bf16[16,128]{1,0:T(8,128)(2,1)S(1)}, bf16[16,128]{1,0:T(8,128)(2,1)S(1)}, u32[]{:S(2)}, u32[]{:S(2)}) collective-permute-start(bf16[16,128]{1,0:T(8,128)(2,1)S(1)} %get-tuple-element.118.step), channel_id=1, source_target_pairs={{0,32},{32,0},{1,33},{33,1},{2,34},{34,2},{3,35},{35,3},{4,36},{36... | collective-permute-start | bytes 12296 | tf_op jit(solution)/shard_map/ppermute | solution.py:512
  55.0 4.2 %collective-permute-done.7.r1.refs_1_ = bf16[2048,128]{1,0:T(8,128)(2,1)S(1)} collective-permute-done((bf16[2048,128]{1,0:T(8,128)(2,1)}, bf16[2048,128]{1,0:T(8,128)(2,1)S(1)}, u32[]{:S(2)}, u32[]{:S(2)}) %collective-permute-start.7) | collective-permute-done | bytes 524320 | tf_op jit(solution)/shard_map/ppermute | solution.py:503
  59.2 1.2 collective-permute-done.8.r3.refs_3_
  60.8 5.5 %collective-permute-start.10 = (bf16[1024,512]{1,0:T(8,128)(2,1)S(1)}, bf16[1024,512]{1,0:T(8,128)(2,1)S(1)}, u32[]{:S(2)}, u32[]{:S(2)}) collective-permute-start(bf16[1024,512]{1,0:T(8,128)(2,1)S(1)} %bitcast.9), channel_id=1, source_target_pairs={{0,32},{32,0},{1,33},{33,1},{2,34},{34,2},{3,35},{35,3},{4,36},{36... | collective-permute-start | bytes 3145736 | tf_op jit(solution)/shard_map/ppermute | solution.py:512
  66.3 2.8 %gram_first_body.1 = (f32[512,1024]{1,0:T(8,128)S(1)}, bf16[512,512]{1,0:T(8,128)(2,1)S(1)}, bf16[1024,512]{1,0:T(8,128)(2,1)S(1)}) custom-call(s32[3]{0:T(128)S(1)} %pad_add_fusion.pos.spare.refs_0_, s32[88]{0:T(128)S(1)} %get-tuple-element.88.tab.refs_1_, bf16[1024,512]{1,0:T(8,128)(2,1)S(1)} %bitcast.10, bf16[2048,128]{1,0:T(8,128)(2,1)} %get-tuple-element.129.r0.refs_0_, ...), custom_call_target="tpu_custom_call" | custom-call | flops 1073741824 | bytes 4194304 | tf_op jit(solution)/shard_map/gram_first_body/pallas_call | solution.py:296
  70.2 3.1 %gram_body.1 = (bf16[2080,128]{1,0:T(8,128)(2,1)}, bf16[2080,128]{1,0:T(8,128)(2,1)}, bf16[2080,128]{1,0:T(8,128)(2,1)}, bf16[2080,128]{1,0:T(8,128)(2,1)}) custom-call(s32[3]{0:T(128)S(1)} %pad_add_fusion.pos.spare.refs_0_, s32[88]{0:T(128)S(1)} %get-tuple-element.88.tab.refs_1_, bf16[1024,512]{1,0:T(8,128)(2,1)S(1)} %bitcast.11, ...), custom_call_target="tpu_custom_call" | custom-call | flops 1073741824 | bytes 4194304 | tf_op jit(solution)/shard_map/gram_body/pallas_call | solution.py:354
  73.5 4.3 %update_body.1 = bf16[1024,512]{1,0:T(8,128)(2,1)} custom-call(s32[3]{0:T(128)S(1)} %pad_add_fusion.pos.spare.refs_0_, s32[88]{0:T(128)S(1)} %get-tuple-element.88.tab.refs_1_, bf16[1024,512]{1,0:T(8,128)(2,1)S(1)} %bitcast.12, bf16[1024,512]{1,0:T(8,128)(2,1)S(1)} %collective-permute-done.10.other, bf16[1024,512]{1,0:T(8,128)(2,1)S(1)} %get-tuple-element.128.right, ...), custom_call_target="tpu_custom_call" | custom-call | flops 2147483648 | bytes 8388608 | tf_op jit(solution)/shard_map/update_body/pallas_call | solution.py:255
  77.8 8.2 %all-to-all-start.1 = ((bf16[32,32,512]{2,1,0:T(8,128)(2,1)}), bf16[32,32,512]{2,1,0:T(8,128)(2,1)S(1)}, u32[]{:S(2)}, u32[]{:S(2)}) async-start(bf16[32,32,512]{2,1,0:T(8,128)(2,1)} %bitcast.15), calls=%async_computation.1 | async-start | bytes 2097152 | tf_op jit(solution)/shard_map/all_to_all | solution.py:517
  86.2 1.5 %collective-permute-start.16 = (bf16[2080,128]{1,0:T(8,128)(2,1)}, bf16[2080,128]{1,0:T(8,128)(2,1)S(1)}, u32[]{:S(2)}, u32[]{:S(2)}) collective-permute-start(bf16[2080,128]{1,0:T(8,128)(2,1)} %get-tuple-element.150), channel_id=1, source_target_pairs={{0,192},{64,128},{128,64},{192,0},{1,193},{65,129},{129,65},{193,1... | collective-permute-start | bytes 1597448 | tf_op jit(solution)/shard_map/ppermute | solution.py:503
  87.7 1.6 %collective-permute-start.17 = (bf16[2080,128]{1,0:T(8,128)(2,1)S(1)}, bf16[2080,128]{1,0:T(8,128)(2,1)S(1)}, u32[]{:S(2)}, u32[]{:S(2)}) collective-permute-start(bf16[2080,128]{1,0:T(8,128)(2,1)S(1)} %copy-done.13), channel_id=1, source_target_pairs={{0,128},{64,192},{128,0},{192,64},{1,129},{65,193},{129,1},{193,65... | collective-permute-start | bytes 1597448 | tf_op jit(solution)/shard_map/ppermute | solution.py:503
  89.4 9.9 %collective-permute-done.15.g1 = bf16[2080,128]{1,0:T(8,128)(2,1)S(1)} collective-permute-done((bf16[2080,128]{1,0:T(8,128)(2,1)}, bf16[2080,128]{1,0:T(8,128)(2,1)S(1)}, u32[]{:S(2)}, u32[]{:S(2)}) %collective-permute-start.15) | collective-permute-done | bytes 532512 | tf_op jit(solution)/shard_map/ppermute | solution.py:503
  100.3 11.5 %collective-permute-done.17.g2 = bf16[2080,128]{1,0:T(8,128)(2,1)S(1)} collective-permute-done((bf16[2080,128]{1,0:T(8,128)(2,1)S(1)}, bf16[2080,128]{1,0:T(8,128)(2,1)S(1)}, u32[]{:S(2)}, u32[]{:S(2)}) %collective-permute-start.17) | collective-permute-done | bytes 532512 | tf_op jit(solution)/shard_map/ppermute | solution.py:503
  112.4 1.4 %collective-permute-start.18 = (bf16[288,512]{1,0:T(8,128)(2,1)S(1)}, bf16[288,512]{1,0:T(8,128)(2,1)S(1)}, u32[]{:S(2)}, u32[]{:S(2)}) collective-permute-start(bf16[288,512]{1,0:T(8,128)(2,1)S(1)} %back_body.1.refs_2_), channel_id=1, source_target_pairs={{0,192},{64,128},{128,64},{192,0},{1,193},{65,129},{129,65},{193,1... | collective-permute-start | bytes 884744 | tf_op jit(solution)/shard_map/ppermute | solution.py:503
  113.8 4.1 %collective-permute-start.22 = (bf16[288,512]{1,0:T(8,128)(2,1)S(1)}, bf16[288,512]{1,0:T(8,128)(2,1)S(1)}, u32[]{:S(2)}, u32[]{:S(2)}) collective-permute-start(bf16[288,512]{1,0:T(8,128)(2,1)S(1)} %back_body.1.refs_2_), channel_id=1, source_target_pairs={{0,32},{32,0},{1,33},{33,1},{2,34},{34,2},{3,35},{35,3},{4,36},{36... | collective-permute-start | bytes 884744 | tf_op jit(solution)/shard_map/ppermute | solution.py:512
  117.9 4.7 %stats_body.1 = (f32[3,128,1024]{2,1,0:T(8,128)}, f32[3,1024,128]{2,1,0:T(8,128)}, bf16[16,1024]{1,0:T(8,128)(2,1)S(1)}) custom-call(s32[3]{0:T(128)S(1)} %pad_add_fusion.pos.spare.refs_0_, s32[88]{0:T(128)S(1)} %get-tuple-element.88.tab.refs_1_, f32[3,128,1024]{2,1,0:T(8,128)} %left.3, f32[3,1024,128]{2,1,0:T(8,128)} %right.3, ...), custom_call_target="tpu_custom_call" | custom-call | bytes 8388608 | tf_op jit(solution)/shard_map/stats_body/pallas_call | solution.py:414
  123.3 1.4 collective-permute-start.23
  125.6 1.4 %collective-permute-start.21 = (bf16[128,512]{1,0:T(8,128)(2,1)S(1)}, bf16[128,512]{1,0:T(8,128)(2,1)S(1)}, u32[]{:S(2)}, u32[]{:S(2)}) collective-permute-start(bf16[128,512]{1,0:T(8,128)(2,1)S(1)} %slice.27), channel_id=1, source_target_pairs={{0,192},{64,128},{128,64},{192,0},{1,193},{65,129},{129,65},{193,1... | collective-permute-start | bytes 393224 | tf_op jit(solution)/shard_map/ppermute | solution.py:503
  127.1 2.0 %place_part.2.refs_6_ = bf16[1152,1024]{1,0:T(8,128)(2,1)} custom-call(s32[3]{0:T(128)S(1)} %pad_add_fusion.pos.spare.refs_0_, s32[88]{0:T(128)S(1)} %get-tuple-element.88.tab.refs_1_, bf16[288,512]{1,0:T(8,128)(2,1)S(1)} %back_body.1.refs_2_, bf16[288,512]{1,0:T(8,128)(2,1)S(1)} %collective-permute-done.22.refs_3_, ...), custom_call_target="tpu_custom_call" | custom-call | bytes 3538944 | tf_op jit(solution)/shard_map/place_part/pallas_call | solution.py:480
  129.0 2.6 %collective-permute-done.21.refs_4_ = bf16[128,512]{1,0:T(8,128)(2,1)S(1)} collective-permute-done((bf16[128,512]{1,0:T(8,128)(2,1)S(1)}, bf16[128,512]{1,0:T(8,128)(2,1)S(1)}, u32[]{:S(2)}, u32[]{:S(2)}) %collective-permute-start.21) | collective-permute-done | bytes 131104 | tf_op jit(solution)/shard_map/ppermute | solution.py:503
  131.7 1.2 collective-permute-start.25
  132.9 1.3 collective-permute-done.26.refs_5_
  134.2 1.4 %place_part.3 = bf16[1152,1024]{1,0:T(8,128)(2,1)} custom-call(s32[3]{0:T(128)S(1)} %pad_add_fusion.pos.spare.refs_0_, s32[88]{0:T(128)S(1)} %get-tuple-element.88.tab.refs_1_, bf16[160,512]{1,0:T(8,128)(2,1)S(1)} %collective-permute-done.20.refs_2_, bf16[160,512]{1,0:T(8,128)(2,1)S(1)} %collective-permute-done.25.refs_3_, ...), custom_call_target="tpu_custom_call", output_to_operand_aliasing={{}: (6, {})} | custom-call | bytes 1179648 | tf_op jit(solution)/shard_map/place_part/pallas_call | solution.py:480
  (74 shorter events, 10.5 us)
Async XLA Ops:
  0.6 7.7 %collective-permute-start = (bf16[1152,1024]{1,0:T(8,128)(2,1)}, bf16[1152,1024]{1,0:T(8,128)(2,1)S(1)}, u32[]{:S(2)}, u32[]{:S(2)}) collective-permute-start(bf16[1152,1024]{1,0:T(8,128)(2,1)} %bitcast.16), channel_id=1, source_target_pairs={{0,32},{32,0},{1,33},{33,1},{2,34},{34,2},{3,35},{35,3},{4,36},{36... | collective-permute-start | bytes 7077896 | tf_op jit(solution)/shard_map/ppermute | solution.py:512
  4.0 4.4 %collective-permute-start.1 = (bf16[1,1,1024]{2,1,0:T(2,128)(2,1)}, bf16[1,1,1024]{2,1,0:T(2,128)(2,1)S(1)}, u32[]{:S(2)}, u32[]{:S(2)}) collective-permute-start(bf16[1,1,1024]{2,1,0:T(2,128)(2,1)} %vec.1), channel_id=1, source_target_pairs={{0,32},{32,0},{1,33},{33,1},{2,34},{34,2},{3,35},{35,3},{4,36},{36... | collective-permute-start | bytes 6152 | tf_op jit(solution)/shard_map/ppermute | solution.py:512
  9.4 9.0 %collective-permute-start.2 = (bf16[320,512]{1,0:T(8,128)(2,1)S(1)}, bf16[320,512]{1,0:T(8,128)(2,1)S(1)}, u32[]{:S(2)}, u32[]{:S(2)}) collective-permute-start(bf16[320,512]{1,0:T(8,128)(2,1)S(1)} %get-tuple-element.92), channel_id=1, source_target_pairs={{0,64},{64,0},{128,192},{192,128},{1,65},{65,1},{129,193},{193,129... | collective-permute-start | bytes 983048 | tf_op jit(solution)/shard_map/ppermute | solution.py:503
  9.5 10.0 %collective-permute-start.4 = (bf16[288,512]{1,0:T(8,128)(2,1)S(1)}, bf16[288,512]{1,0:T(8,128)(2,1)S(1)}, u32[]{:S(2)}, u32[]{:S(2)}) collective-permute-start(bf16[288,512]{1,0:T(8,128)(2,1)S(1)} %get-tuple-element.94), channel_id=1, source_target_pairs={{0,192},{64,128},{128,64},{192,0},{1,193},{65,129},{129,65},{193,1... | collective-permute-start | bytes 884744 | tf_op jit(solution)/shard_map/ppermute | solution.py:503
  18.4 5.8 %collective-permute-start.3 = (bf16[160,512]{1,0:T(8,128)(2,1)S(1)}, bf16[160,512]{1,0:T(8,128)(2,1)S(1)}, u32[]{:S(2)}, u32[]{:S(2)}) collective-permute-start(bf16[160,512]{1,0:T(8,128)(2,1)S(1)} %slice_add_fusion), channel_id=1, source_target_pairs={{0,192},{64,128},{128,64},{192,0},{1,193},{65,129},{129,65},{193,1... | collective-permute-start | bytes 491528 | tf_op jit(solution)/shard_map/ppermute | solution.py:503
  19.5 4.1 %collective-permute-start.5 = (bf16[144,512]{1,0:T(8,128)(2,1)S(1)}, bf16[144,512]{1,0:T(8,128)(2,1)S(1)}, u32[]{:S(2)}, u32[]{:S(2)}) collective-permute-start(bf16[144,512]{1,0:T(8,128)(2,1)S(1)} %slice_add_fusion.1), channel_id=1, source_target_pairs={{0,64},{64,0},{128,192},{192,128},{1,65},{65,1},{129,193},{193,129... | collective-permute-start | bytes 442376 | tf_op jit(solution)/shard_map/ppermute | solution.py:503
  25.9 34.9 %all-to-all-start = ((bf16[32,32,512]{2,1,0:T(8,128)(2,1)}), bf16[32,32,512]{2,1,0:T(8,128)(2,1)S(1)}, u32[]{:S(2)}, u32[]{:S(2)}) async-start(bf16[32,32,512]{2,1,0:T(8,128)(2,1)} %bitcast.18), calls=%async_computation | async-start | bytes 2097152 | tf_op jit(solution)/shard_map/all_to_all | solution.py:517
  36.7 32.4 %copy-start.9 = (bf16[2048,128]{1,0:T(8,128)(2,1)S(1)}, bf16[2048,128]{1,0:T(8,128)(2,1)}, u32[]{:S(2)}) copy-start(bf16[2048,128]{1,0:T(8,128)(2,1)} %get-tuple-element.129.r0.refs_0_) | copy-start | bytes 1572868
  36.7 12.4 %collective-permute-start.6 = (bf16[2048,128]{1,0:T(8,128)(2,1)S(1)}, bf16[2048,128]{1,0:T(8,128)(2,1)S(1)}, u32[]{:S(2)}, u32[]{:S(2)}) collective-permute-start(bf16[2048,128]{1,0:T(8,128)(2,1)S(1)} %copy-done.14), channel_id=1, source_target_pairs={{0,128},{64,192},{128,0},{192,64},{1,129},{65,193},{129,1},{193,65... | collective-permute-start | bytes 1572872 | tf_op jit(solution)/shard_map/ppermute | solution.py:503
  49.1 10.1 %collective-permute-start.7 = (bf16[2048,128]{1,0:T(8,128)(2,1)}, bf16[2048,128]{1,0:T(8,128)(2,1)S(1)}, u32[]{:S(2)}, u32[]{:S(2)}) collective-permute-start(bf16[2048,128]{1,0:T(8,128)(2,1)} %get-tuple-element.115), channel_id=1, source_target_pairs={{0,64},{64,0},{128,192},{192,128},{1,65},{65,1},{129,193},{193,129... | collective-permute-start | bytes 1572872 | tf_op jit(solution)/shard_map/ppermute | solution.py:503
  49.2 11.2 %collective-permute-start.8 = (bf16[2048,128]{1,0:T(8,128)(2,1)}, bf16[2048,128]{1,0:T(8,128)(2,1)S(1)}, u32[]{:S(2)}, u32[]{:S(2)}) collective-permute-start(bf16[2048,128]{1,0:T(8,128)(2,1)} %get-tuple-element.117), channel_id=1, source_target_pairs={{0,192},{64,128},{128,64},{192,0},{1,193},{65,129},{129,65},{193,1... | collective-permute-start | bytes 1572872 | tf_op jit(solution)/shard_map/ppermute | solution.py:503
  50.6 4.4 %collective-permute-start.9 = (bf16[16,128]{1,0:T(8,128)(2,1)S(1)}, bf16[16,128]{1,0:T(8,128)(2,1)S(1)}, u32[]{:S(2)}, u32[]{:S(2)}) collective-permute-start(bf16[16,128]{1,0:T(8,128)(2,1)S(1)} %get-tuple-element.118.step), channel_id=1, source_target_pairs={{0,32},{32,0},{1,33},{33,1},{2,34},{34,2},{3,35},{35,3},{4,36},{36... | collective-permute-start | bytes 12296 | tf_op jit(solution)/shard_map/ppermute | solution.py:512
  60.8 8.2 %collective-permute-start.10 = (bf16[1024,512]{1,0:T(8,128)(2,1)S(1)}, bf16[1024,512]{1,0:T(8,128)(2,1)S(1)}, u32[]{:S(2)}, u32[]{:S(2)}) collective-permute-start(bf16[1024,512]{1,0:T(8,128)(2,1)S(1)} %bitcast.9), channel_id=1, source_target_pairs={{0,32},{32,0},{1,33},{33,1},{2,34},{34,2},{3,35},{35,3},{4,36},{36... | collective-permute-start | bytes 3145736 | tf_op jit(solution)/shard_map/ppermute | solution.py:512
  69.1 4.3 %collective-permute-start.11 = (bf16[2048,128]{1,0:T(8,128)(2,1)S(1)}, bf16[2048,128]{1,0:T(8,128)(2,1)S(1)}, u32[]{:S(2)}, u32[]{:S(2)}) collective-permute-start(bf16[2048,128]{1,0:T(8,128)(2,1)S(1)} %copy-done.9), channel_id=1, source_target_pairs={{0,32},{32,0},{1,33},{33,1},{2,34},{34,2},{3,35},{35,3},{4,36},{36... | collective-permute-start | bytes 1572872 | tf_op jit(solution)/shard_map/ppermute | solution.py:512
  69.2 4.2 %collective-permute-start.12 = (bf16[2048,128]{1,0:T(8,128)(2,1)}, bf16[2048,128]{1,0:T(8,128)(2,1)S(1)}, u32[]{:S(2)}, u32[]{:S(2)}) collective-permute-start(bf16[2048,128]{1,0:T(8,128)(2,1)} %copy-done.11), channel_id=1, source_target_pairs={{0,32},{32,0},{1,33},{33,1},{2,34},{34,2},{3,35},{35,3},{4,36},{36... | collective-permute-start | bytes 1572872 | tf_op jit(solution)/shard_map/ppermute | solution.py:512
  69.7 3.7 %collective-permute-start.13 = (bf16[2048,128]{1,0:T(8,128)(2,1)}, bf16[2048,128]{1,0:T(8,128)(2,1)S(1)}, u32[]{:S(2)}, u32[]{:S(2)}) collective-permute-start(bf16[2048,128]{1,0:T(8,128)(2,1)} %copy-done.10), channel_id=1, source_target_pairs={{0,32},{32,0},{1,33},{33,1},{2,34},{34,2},{3,35},{35,3},{4,36},{36... | collective-permute-start | bytes 1572872 | tf_op jit(solution)/shard_map/ppermute | solution.py:512
  69.8 3.8 %collective-permute-start.14 = (bf16[2048,128]{1,0:T(8,128)(2,1)}, bf16[2048,128]{1,0:T(8,128)(2,1)S(1)}, u32[]{:S(2)}, u32[]{:S(2)}) collective-permute-start(bf16[2048,128]{1,0:T(8,128)(2,1)} %copy-done.12), channel_id=1, source_target_pairs={{0,32},{32,0},{1,33},{33,1},{2,34},{34,2},{3,35},{35,3},{4,36},{36... | collective-permute-start | bytes 1572872 | tf_op jit(solution)/shard_map/ppermute | solution.py:512
  77.8 34.0 %all-to-all-start.1 = ((bf16[32,32,512]{2,1,0:T(8,128)(2,1)}), bf16[32,32,512]{2,1,0:T(8,128)(2,1)S(1)}, u32[]{:S(2)}, u32[]{:S(2)}) async-start(bf16[32,32,512]{2,1,0:T(8,128)(2,1)} %bitcast.15), calls=%async_computation.1 | async-start | bytes 2097152 | tf_op jit(solution)/shard_map/all_to_all | solution.py:517
  86.0 13.3 %collective-permute-start.15 = (bf16[2080,128]{1,0:T(8,128)(2,1)}, bf16[2080,128]{1,0:T(8,128)(2,1)S(1)}, u32[]{:S(2)}, u32[]{:S(2)}) collective-permute-start(bf16[2080,128]{1,0:T(8,128)(2,1)} %get-tuple-element.149), channel_id=1, source_target_pairs={{0,64},{64,0},{128,192},{192,128},{1,65},{65,1},{129,193},{193,129... | collective-permute-start | bytes 1597448 | tf_op jit(solution)/shard_map/ppermute | solution.py:503
  86.2 14.1 %collective-permute-start.16 = (bf16[2080,128]{1,0:T(8,128)(2,1)}, bf16[2080,128]{1,0:T(8,128)(2,1)S(1)}, u32[]{:S(2)}, u32[]{:S(2)}) collective-permute-start(bf16[2080,128]{1,0:T(8,128)(2,1)} %get-tuple-element.150), channel_id=1, source_target_pairs={{0,192},{64,128},{128,64},{192,0},{1,193},{65,129},{129,65},{193,1... | collective-permute-start | bytes 1597448 | tf_op jit(solution)/shard_map/ppermute | solution.py:503
  87.7 24.1 %collective-permute-start.17 = (bf16[2080,128]{1,0:T(8,128)(2,1)S(1)}, bf16[2080,128]{1,0:T(8,128)(2,1)S(1)}, u32[]{:S(2)}, u32[]{:S(2)}) collective-permute-start(bf16[2080,128]{1,0:T(8,128)(2,1)S(1)} %copy-done.13), channel_id=1, source_target_pairs={{0,128},{64,192},{128,0},{192,64},{1,129},{65,193},{129,1},{193,65... | collective-permute-start | bytes 1597448 | tf_op jit(solution)/shard_map/ppermute | solution.py:503
  99.3 18.6 %copy-start.6 = (bf16[2080,128]{1,0:T(8,128)(2,1)}, bf16[2080,128]{1,0:T(8,128)(2,1)S(1)}, u32[]{:S(2)}) copy-start(bf16[2080,128]{1,0:T(8,128)(2,1)S(1)} %collective-permute-done.15.g1) | copy-start | bytes 1597444
  100.3 17.6 %copy-start.7 = (bf16[2080,128]{1,0:T(8,128)(2,1)}, bf16[2080,128]{1,0:T(8,128)(2,1)S(1)}, u32[]{:S(2)}) copy-start(bf16[2080,128]{1,0:T(8,128)(2,1)S(1)} %collective-permute-done.16.g3) | copy-start | bytes 1597444
  112.4 10.8 %collective-permute-start.18 = (bf16[288,512]{1,0:T(8,128)(2,1)S(1)}, bf16[288,512]{1,0:T(8,128)(2,1)S(1)}, u32[]{:S(2)}, u32[]{:S(2)}) collective-permute-start(bf16[288,512]{1,0:T(8,128)(2,1)S(1)} %back_body.1.refs_2_), channel_id=1, source_target_pairs={{0,192},{64,128},{128,64},{192,0},{1,193},{65,129},{129,65},{193,1... | collective-permute-start | bytes 884744 | tf_op jit(solution)/shard_map/ppermute | solution.py:503
  113.8 9.4 %collective-permute-start.19 = (bf16[288,512]{1,0:T(8,128)(2,1)S(1)}, bf16[288,512]{1,0:T(8,128)(2,1)S(1)}, u32[]{:S(2)}, u32[]{:S(2)}) collective-permute-start(bf16[288,512]{1,0:T(8,128)(2,1)S(1)} %back_body.1.refs_2_), channel_id=1, source_target_pairs={{0,64},{64,0},{128,192},{192,128},{1,65},{65,1},{129,193},{193,129... | collective-permute-start | bytes 884744 | tf_op jit(solution)/shard_map/ppermute | solution.py:503
  113.8 13.2 %collective-permute-start.22 = (bf16[288,512]{1,0:T(8,128)(2,1)S(1)}, bf16[288,512]{1,0:T(8,128)(2,1)S(1)}, u32[]{:S(2)}, u32[]{:S(2)}) collective-permute-start(bf16[288,512]{1,0:T(8,128)(2,1)S(1)} %back_body.1.refs_2_), channel_id=1, source_target_pairs={{0,32},{32,0},{1,33},{33,1},{2,34},{34,2},{3,35},{35,3},{4,36},{36... | collective-permute-start | bytes 884744 | tf_op jit(solution)/shard_map/ppermute | solution.py:512
  123.3 3.8 %collective-permute-start.23 = (bf16[288,512]{1,0:T(8,128)(2,1)S(1)}, bf16[288,512]{1,0:T(8,128)(2,1)S(1)}, u32[]{:S(2)}, u32[]{:S(2)}) collective-permute-start(bf16[288,512]{1,0:T(8,128)(2,1)S(1)} %collective-permute-done.18.refs_4_), channel_id=1, source_target_pairs={{0,32},{32,0},{1,33},{33,1},{2,34},{34,2},{3,35},{35,3},{4,36},{36... | collective-permute-start | bytes 884744 | tf_op jit(solution)/shard_map/ppermute | solution.py:512
  124.6 2.4 %collective-permute-start.24 = (bf16[288,512]{1,0:T(8,128)(2,1)S(1)}, bf16[288,512]{1,0:T(8,128)(2,1)S(1)}, u32[]{:S(2)}, u32[]{:S(2)}) collective-permute-start(bf16[288,512]{1,0:T(8,128)(2,1)S(1)} %collective-permute-done.19.refs_6_), channel_id=1, source_target_pairs={{0,32},{32,0},{1,33},{33,1},{2,34},{34,2},{3,35},{35,3},{4,36},{36... | collective-permute-start | bytes 884744 | tf_op jit(solution)/shard_map/ppermute | solution.py:512
  124.6 7.0 %collective-permute-start.20 = (bf16[160,512]{1,0:T(8,128)(2,1)S(1)}, bf16[160,512]{1,0:T(8,128)(2,1)S(1)}, u32[]{:S(2)}, u32[]{:S(2)}) collective-permute-start(bf16[160,512]{1,0:T(8,128)(2,1)S(1)} %slice.26), channel_id=1, source_target_pairs={{0,64},{64,0},{128,192},{192,128},{1,65},{65,1},{129,193},{193,129... | collective-permute-start | bytes 491528 | tf_op jit(solution)/shard_map/ppermute | solution.py:503
  125.6 6.0 %collective-permute-start.21 = (bf16[128,512]{1,0:T(8,128)(2,1)S(1)}, bf16[128,512]{1,0:T(8,128)(2,1)S(1)}, u32[]{:S(2)}, u32[]{:S(2)}) collective-permute-start(bf16[128,512]{1,0:T(8,128)(2,1)S(1)} %slice.27), channel_id=1, source_target_pairs={{0,192},{64,128},{128,64},{192,0},{1,193},{65,129},{129,65},{193,1... | collective-permute-start | bytes 393224 | tf_op jit(solution)/shard_map/ppermute | solution.py:503
  131.7 2.5 %collective-permute-start.25 = (bf16[160,512]{1,0:T(8,128)(2,1)S(1)}, bf16[160,512]{1,0:T(8,128)(2,1)S(1)}, u32[]{:S(2)}, u32[]{:S(2)}) collective-permute-start(bf16[160,512]{1,0:T(8,128)(2,1)S(1)} %collective-permute-done.20.refs_2_), channel_id=1, source_target_pairs={{0,32},{32,0},{1,33},{33,1},{2,34},{34,2},{3,35},{35,3},{4,36},{36... | collective-permute-start | bytes 491528 | tf_op jit(solution)/shard_map/ppermute | solution.py:512
  132.9 1.3 collective-permute-start.26
  (12 other events, 143.3 us)
where the time goes:
time: 136 us
  waiting for transfers between devices  55.4 us (41%)
  starting transfers between devices  51 us (38%)
  Pallas kernels  26.8 us (20%)
    ppermute x14, waiting for transfers between devices, hop(): return lax.ppermute(x, 'y', [(i, i ^ k) for i in range(RING)])  52.5 us
    ppermute x13, starting transfers between devices, swap(): return lax.ppermute(x, 'core', [(0, 1), (1, 0)])  20.2 us
    all_to_all x2, starting transfers between devices, route(): return lax.all_to_all(x, ('x', 'z'), 0, 0).reshape(BLOCK, HALF)  18.9 us
    ppermute x14, starting transfers between devices, hop(): return lax.ppermute(x, 'y', [(i, i ^ k) for i in range(RING)])  11.8 us
    pallas_call x1, Pallas kernels, stats(): call(stats_body, (), [outside()] * (2 + RING), [outside(), outside(), who...  4.75 us
    pallas_call x1, Pallas kernels, update(): call(update_body, (), [whole()] * 3 + [outside()] * (2 * RING), outside()...  4.25 us
    pallas_call x2, Pallas kernels, place(): pl.pallas_call(place_part, name='place_part', grid_spec=pltpu.PrefetchSca...  3.42 us
    pallas_call x1, Pallas kernels, front(): call(front_body, (), [smem, outside(), outside()], [smem, whole(), whole(...  3.27 us
  transfers between devices with their start and end apart: 29, of which 15 were waited for; matrix products, arithmetic and copies ran while one was open for 1% of the time, Pallas kernels for 13%

commit v1 on v0

--- a/solution.py
+++ b/solution.py
@@ -503,11 +503,6 @@
     return lax.ppermute(x, "y", [(i, i ^ k) for i in range(RING)])
 
 
-def spread(x):
-    far, near, other = lax.optimization_barrier((hop(x[2], 2), x[1], x[3]))
-    return [x[0], hop(near, 1), far, hop(other, 3)]
-
-
 def swap(x):
     return lax.ppermute(x, "core", [(0, 1), (1, 0)])
 
@@ -548,10 +543,13 @@
         pos, tab, parts, vec_param, vec_first, vec_second, decay_mask
     )
     send, sides = lax.optimization_barrier((send, sides))
-    sides = spread(sides)
+    near, other_near, far = hop(sides[1], 1), hop(sides[3], 3), hop(sides[2], 2)
     mine = route(send)
     step_other = swap(step)
-    mine, sides, step_other = lax.optimization_barrier((mine, sides, step_other))
+    mine, near, other_near, far, step_other = lax.optimization_barrier(
+        (mine, near, other_near, far, step_other)
+    )
+    sides = [sides[0], near, far, other_near]
     other = swap(mine)
     across, down, right = gram_first(pos, tab, mine, sides)
     other, sides, across, down, right = lax.optimization_barrier(

time: 136 us -> 135 us (level)
    ppermute x14, starting transfers between devices: 11.8 us -> 13.3 us  [hop(): return lax.ppermute(x, 'y', [(i, i ^ k) for i in range(RING)])]
    ppermute x14, waiting for transfers between devices: 52.5 us -> 51 us  [hop(): return lax.ppermute(x, 'y', [(i, i ^ k) for i in range(RING)])]
where the time goes in v1:
time: 135 us
  waiting for transfers between devices  54.1 us (40%)
  starting transfers between devices  51.6 us (38%)
  Pallas kernels  26.8 us (20%)
    ppermute x14, waiting for transfers between devices, hop(): return lax.ppermute(x, 'y', [(i, i ^ k) for i in range(RING)])  51 us
    ppermute x13, starting transfers between devices, swap(): return lax.ppermute(x, 'core', [(0, 1), (1, 0)])  20 us
    all_to_all x2, starting transfers between devices, route(): return lax.all_to_all(x, ('x', 'z'), 0, 0).reshape(BLOCK, HALF)  18.3 us
    ppermute x14, starting transfers between devices, hop(): return lax.ppermute(x, 'y', [(i, i ^ k) for i in range(RING)])  13.3 us
    pallas_call x1, Pallas kernels, stats(): call(stats_body, (), [outside()] * (2 + RING), [outside(), outside(), who...  4.75 us
    pallas_call x1, Pallas kernels, update(): call(update_body, (), [whole()] * 3 + [outside()] * (2 * RING), outside()...  4.26 us
    pallas_call x2, Pallas kernels, place(): pl.pallas_call(place_part, name='place_part', grid_spec=pltpu.PrefetchSca...  3.42 us
    pallas_call x1, Pallas kernels, front(): call(front_body, (), [smem, outside(), outside()], [smem, whole(), whole(...  3.27 us
  transfers between devices with their start and end apart: 29, of which 15 were waited for; matrix products, arithmetic and copies ran while one was open for 1% of the time, Pallas kernels for 13%

profile of v1, /device:TPU:1, one launch (start us, length us, event | category | flops | bytes accessed | tf_op | source)
XLA Modules:
  0.0 135.1 jit_solution(16015324910776144257)
XLA Ops:
  0.6 3.3 %collective-permute-start = (bf16[1152,1024]{1,0:T(8,128)(2,1)}, bf16[1152,1024]{1,0:T(8,128)(2,1)S(1)}, u32[]{:S(2)}, u32[]{:S(2)}) collective-permute-start(bf16[1152,1024]{1,0:T(8,128)(2,1)} %bitcast.16), channel_id=1, source_target_pairs={{0,32},{32,0},{1,33},{33,1},{2,34},{34,2},{3,35},{35,3},{4,36},{36... | collective-permute-start | bytes 7077896 | tf_op jit(solution)/shard_map/ppermute | solution.py:507
  4.9 3.3 %front_body.1 = (s32[88]{0:T(128)S(1)}, bf16[4,1152,128]{2,1,0:T(8,128)(2,1)S(1)}, bf16[1,1,1024]{2,1,0:T(2,128)(2,1)S(1)}) custom-call(s32[3]{0:T(128)S(1)} %pad_add_fusion.pos.spare.refs_0_, s32[3]{0:T(128)S(1)} %pad_add_fusion.pos.spare.refs_0_, s32[72]{0:T(128)S(1)} %pad_add_fusion.1.maps, bf16[1152,1024]{1,0:T(8,128)(2,1)} %bitcast.17, ...), custom_call_target="tpu_custom_call" | custom-call | bytes 2359296 | tf_op jit(solution)/shard_map/front_body/pallas_call | solution.py:119
  9.5 1.4 %collective-permute-start.4 = (bf16[288,512]{1,0:T(8,128)(2,1)S(1)}, bf16[288,512]{1,0:T(8,128)(2,1)S(1)}, u32[]{:S(2)}, u32[]{:S(2)}) collective-permute-start(bf16[288,512]{1,0:T(8,128)(2,1)S(1)} %get-tuple-element.90), channel_id=1, source_target_pairs={{0,192},{64,128},{128,64},{192,0},{1,193},{65,129},{129,65},{193,1... | collective-permute-start | bytes 884744 | tf_op jit(solution)/shard_map/ppermute | solution.py:503
  10.9 7.5 %collective-permute-done.2.a1 = bf16[320,512]{1,0:T(8,128)(2,1)S(1)} collective-permute-done((bf16[320,512]{1,0:T(8,128)(2,1)S(1)}, bf16[320,512]{1,0:T(8,128)(2,1)S(1)}, u32[]{:S(2)}, u32[]{:S(2)}) %collective-permute-start.2) | collective-permute-done | bytes 327712 | tf_op jit(solution)/shard_map/ppermute | solution.py:503
  19.6 2.0 %roots_body.1 = (bf16[2048,128]{1,0:T(8,128)(2,1)}, bf16[2048,128]{1,0:T(8,128)(2,1)}, bf16[2048,128]{1,0:T(8,128)(2,1)}, bf16[2048,128]{1,0:T(8,128)(2,1)}) custom-call(s32[3]{0:T(128)S(1)} %pad_add_fusion.pos.spare.refs_0_, s32[88]{0:T(128)S(1)} %get-tuple-element.84.tab.refs_1_, bf16[3,1024,128]{2,1,0:T(8,128)(2,1)S(1)} %copy-done, ...), custom_call_target="tpu_custom_call" | custom-call | bytes 3670016 | tf_op jit(solution)/shard_map/roots_body/pallas_call | solution.py:216
  21.6 2.0 %collective-permute-done.5.b2 = bf16[144,512]{1,0:T(8,128)(2,1)S(1)} collective-permute-done((bf16[144,512]{1,0:T(8,128)(2,1)S(1)}, bf16[144,512]{1,0:T(8,128)(2,1)S(1)}, u32[]{:S(2)}, u32[]{:S(2)}) %collective-permute-start.5) | collective-permute-done | bytes 147488 | tf_op jit(solution)/shard_map/ppermute | solution.py:503
  24.2 1.7 %total_body.1 = (bf16[1024,512]{1,0:T(8,128)(2,1)}, f32[1,128]{1,0:T(1,128)}, f32[1,128]{1,0:T(1,128)}, bf16[16,128]{1,0:T(8,128)(2,1)S(1)}) custom-call(s32[3]{0:T(128)S(1)} %pad_add_fusion.pos.spare.refs_0_, s32[88]{0:T(128)S(1)} %get-tuple-element.84.tab.refs_1_, bf16[320,512]{1,0:T(8,128)(2,1)S(1)} %get-tuple-element.95.a0, ...), custom_call_target="tpu_custom_call" | custom-call | bytes 2818048 | tf_op jit(solution)/shard_map/total_body/pallas_call | solution.py:190
  25.9 10.7 %all-to-all-start = ((bf16[32,32,512]{2,1,0:T(8,128)(2,1)}), bf16[32,32,512]{2,1,0:T(8,128)(2,1)S(1)}, u32[]{:S(2)}, u32[]{:S(2)}) async-start(bf16[32,32,512]{2,1,0:T(8,128)(2,1)} %bitcast.18), calls=%async_computation | async-start | bytes 2097152 | tf_op jit(solution)/shard_map/all_to_all | solution.py:512
  36.8 1.4 %collective-permute-start.7 = (bf16[2048,128]{1,0:T(8,128)(2,1)}, bf16[2048,128]{1,0:T(8,128)(2,1)S(1)}, u32[]{:S(2)}, u32[]{:S(2)}) collective-permute-start(bf16[2048,128]{1,0:T(8,128)(2,1)} %get-tuple-element.108), channel_id=1, source_target_pairs={{0,192},{64,128},{128,64},{192,0},{1,193},{65,129},{129,65},{193,1... | collective-permute-start | bytes 1572872 | tf_op jit(solution)/shard_map/ppermute | solution.py:503
  38.1 1.9 %collective-permute-start.8 = (bf16[2048,128]{1,0:T(8,128)(2,1)}, bf16[2048,128]{1,0:T(8,128)(2,1)S(1)}, u32[]{:S(2)}, u32[]{:S(2)}) collective-permute-start(bf16[2048,128]{1,0:T(8,128)(2,1)} %get-tuple-element.109), channel_id=1, source_target_pairs={{0,128},{64,192},{128,0},{192,64},{1,129},{65,193},{129,1},{193,65... | collective-permute-start | bytes 1572872 | tf_op jit(solution)/shard_map/ppermute | solution.py:503
  40.0 3.4 %collective-permute-start.9 = (bf16[16,128]{1,0:T(8,128)(2,1)S(1)}, bf16[16,128]{1,0:T(8,128)(2,1)S(1)}, u32[]{:S(2)}, u32[]{:S(2)}) collective-permute-start(bf16[16,128]{1,0:T(8,128)(2,1)S(1)} %get-tuple-element.110.step), channel_id=1, source_target_pairs={{0,32},{32,0},{1,33},{33,1},{2,34},{34,2},{3,35},{35,3},{4,36},{36... | collective-permute-start | bytes 12296 | tf_op jit(solution)/shard_map/ppermute | solution.py:507
  44.3 3.5 %collective-permute-done.6.r1.refs_1_ = bf16[2048,128]{1,0:T(8,128)(2,1)S(1)} collective-permute-done((bf16[2048,128]{1,0:T(8,128)(2,1)}, bf16[2048,128]{1,0:T(8,128)(2,1)S(1)}, u32[]{:S(2)}, u32[]{:S(2)}) %collective-permute-start.6) | collective-permute-done | bytes 524320 | tf_op jit(solution)/shard_map/ppermute | solution.py:503
  47.8 1.3 collective-permute-done.7.r3.refs_3_
  49.1 11.2 %collective-permute-done.8.r2.refs_2_ = bf16[2048,128]{1,0:T(8,128)(2,1)S(1)} collective-permute-done((bf16[2048,128]{1,0:T(8,128)(2,1)}, bf16[2048,128]{1,0:T(8,128)(2,1)S(1)}, u32[]{:S(2)}, u32[]{:S(2)}) %collective-permute-start.8) | collective-permute-done | bytes 524320 | tf_op jit(solution)/shard_map/ppermute | solution.py:503
  60.8 5.5 %collective-permute-start.10 = (bf16[1024,512]{1,0:T(8,128)(2,1)S(1)}, bf16[1024,512]{1,0:T(8,128)(2,1)S(1)}, u32[]{:S(2)}, u32[]{:S(2)}) collective-permute-start(bf16[1024,512]{1,0:T(8,128)(2,1)S(1)} %bitcast.9), channel_id=1, source_target_pairs={{0,32},{32,0},{1,33},{33,1},{2,34},{34,2},{3,35},{35,3},{4,36},{36... | collective-permute-start | bytes 3145736 | tf_op jit(solution)/shard_map/ppermute | solution.py:507
  66.3 2.8 %gram_first_body.1 = (f32[512,1024]{1,0:T(8,128)S(1)}, bf16[512,512]{1,0:T(8,128)(2,1)S(1)}, bf16[1024,512]{1,0:T(8,128)(2,1)S(1)}) custom-call(s32[3]{0:T(128)S(1)} %pad_add_fusion.pos.spare.refs_0_, s32[88]{0:T(128)S(1)} %get-tuple-element.84.tab.refs_1_, bf16[1024,512]{1,0:T(8,128)(2,1)S(1)} %bitcast.10, bf16[2048,128]{1,0:T(8,128)(2,1)} %get-tuple-element.121.r0.refs_0_, ...), custom_call_target="tpu_custom_call" | custom-call | flops 1073741824 | bytes 4194304 | tf_op jit(solution)/shard_map/gram_first_body/pallas_call | solution.py:296
  70.2 3.1 %gram_body.1 = (bf16[2080,128]{1,0:T(8,128)(2,1)}, bf16[2080,128]{1,0:T(8,128)(2,1)}, bf16[2080,128]{1,0:T(8,128)(2,1)}, bf16[2080,128]{1,0:T(8,128)(2,1)}) custom-call(s32[3]{0:T(128)S(1)} %pad_add_fusion.pos.spare.refs_0_, s32[88]{0:T(128)S(1)} %get-tuple-element.84.tab.refs_1_, bf16[1024,512]{1,0:T(8,128)(2,1)S(1)} %bitcast.11, ...), custom_call_target="tpu_custom_call" | custom-call | flops 1073741824 | bytes 4194304 | tf_op jit(solution)/shard_map/gram_body/pallas_call | solution.py:354
  73.5 4.3 %update_body.1 = bf16[1024,512]{1,0:T(8,128)(2,1)} custom-call(s32[3]{0:T(128)S(1)} %pad_add_fusion.pos.spare.refs_0_, s32[88]{0:T(128)S(1)} %get-tuple-element.84.tab.refs_1_, bf16[1024,512]{1,0:T(8,128)(2,1)S(1)} %bitcast.12, bf16[1024,512]{1,0:T(8,128)(2,1)S(1)} %collective-permute-done.10.other, bf16[1024,512]{1,0:T(8,128)(2,1)S(1)} %get-tuple-element.120.right, ...), custom_call_target="tpu_custom_call" | custom-call | flops 2147483648 | bytes 8388608 | tf_op jit(solution)/shard_map/update_body/pallas_call | solution.py:255
  77.8 7.5 %all-to-all-start.1 = ((bf16[32,32,512]{2,1,0:T(8,128)(2,1)}), bf16[32,32,512]{2,1,0:T(8,128)(2,1)S(1)}, u32[]{:S(2)}, u32[]{:S(2)}) async-start(bf16[32,32,512]{2,1,0:T(8,128)(2,1)} %bitcast.15), calls=%async_computation.1 | async-start | bytes 2097152 | tf_op jit(solution)/shard_map/all_to_all | solution.py:512
  85.6 1.3 collective-permute-start.16
  86.9 1.8 %collective-permute-start.17 = (bf16[2080,128]{1,0:T(8,128)(2,1)S(1)}, bf16[2080,128]{1,0:T(8,128)(2,1)S(1)}, u32[]{:S(2)}, u32[]{:S(2)}) collective-permute-start(bf16[2080,128]{1,0:T(8,128)(2,1)S(1)} %copy-done.13), channel_id=1, source_target_pairs={{0,128},{64,192},{128,0},{192,64},{1,129},{65,193},{129,1},{193,65... | collective-permute-start | bytes 1597448 | tf_op jit(solution)/shard_map/ppermute | solution.py:503
  88.7 9.9 %collective-permute-done.15.g1 = bf16[2080,128]{1,0:T(8,128)(2,1)S(1)} collective-permute-done((bf16[2080,128]{1,0:T(8,128)(2,1)}, bf16[2080,128]{1,0:T(8,128)(2,1)S(1)}, u32[]{:S(2)}, u32[]{:S(2)}) %collective-permute-start.15) | collective-permute-done | bytes 532512 | tf_op jit(solution)/shard_map/ppermute | solution.py:503
  99.7 11.4 %collective-permute-done.17.g2 = bf16[2080,128]{1,0:T(8,128)(2,1)S(1)} collective-permute-done((bf16[2080,128]{1,0:T(8,128)(2,1)S(1)}, bf16[2080,128]{1,0:T(8,128)(2,1)S(1)}, u32[]{:S(2)}, u32[]{:S(2)}) %collective-permute-start.17) | collective-permute-done | bytes 532512 | tf_op jit(solution)/shard_map/ppermute | solution.py:503
  111.7 1.5 %collective-permute-start.18 = (bf16[288,512]{1,0:T(8,128)(2,1)S(1)}, bf16[288,512]{1,0:T(8,128)(2,1)S(1)}, u32[]{:S(2)}, u32[]{:S(2)}) collective-permute-start(bf16[288,512]{1,0:T(8,128)(2,1)S(1)} %back_body.1.refs_2_), channel_id=1, source_target_pairs={{0,192},{64,128},{128,64},{192,0},{1,193},{65,129},{129,65},{193,1... | collective-permute-start | bytes 884744 | tf_op jit(solution)/shard_map/ppermute | solution.py:503
  113.2 4.0 %collective-permute-start.22 = (bf16[288,512]{1,0:T(8,128)(2,1)S(1)}, bf16[288,512]{1,0:T(8,128)(2,1)S(1)}, u32[]{:S(2)}, u32[]{:S(2)}) collective-permute-start(bf16[288,512]{1,0:T(8,128)(2,1)S(1)} %back_body.1.refs_2_), channel_id=1, source_target_pairs={{0,32},{32,0},{1,33},{33,1},{2,34},{34,2},{3,35},{35,3},{4,36},{36... | collective-permute-start | bytes 884744 | tf_op jit(solution)/shard_map/ppermute | solution.py:507
  117.1 4.7 %stats_body.1 = (f32[3,128,1024]{2,1,0:T(8,128)}, f32[3,1024,128]{2,1,0:T(8,128)}, bf16[16,1024]{1,0:T(8,128)(2,1)S(1)}) custom-call(s32[3]{0:T(128)S(1)} %pad_add_fusion.pos.spare.refs_0_, s32[88]{0:T(128)S(1)} %get-tuple-element.84.tab.refs_1_, f32[3,128,1024]{2,1,0:T(8,128)} %left.3, f32[3,1024,128]{2,1,0:T(8,128)} %right.3, ...), custom_call_target="tpu_custom_call" | custom-call | bytes 8388608 | tf_op jit(solution)/shard_map/stats_body/pallas_call | solution.py:414
  122.5 1.4 collective-permute-start.23
  124.9 1.5 %collective-permute-start.21 = (bf16[128,512]{1,0:T(8,128)(2,1)S(1)}, bf16[128,512]{1,0:T(8,128)(2,1)S(1)}, u32[]{:S(2)}, u32[]{:S(2)}) collective-permute-start(bf16[128,512]{1,0:T(8,128)(2,1)S(1)} %slice.27), channel_id=1, source_target_pairs={{0,192},{64,128},{128,64},{192,0},{1,193},{65,129},{129,65},{193,1... | collective-permute-start | bytes 393224 | tf_op jit(solution)/shard_map/ppermute | solution.py:503
  126.4 2.0 %place_part.2.refs_6_ = bf16[1152,1024]{1,0:T(8,128)(2,1)} custom-call(s32[3]{0:T(128)S(1)} %pad_add_fusion.pos.spare.refs_0_, s32[88]{0:T(128)S(1)} %get-tuple-element.84.tab.refs_1_, bf16[288,512]{1,0:T(8,128)(2,1)S(1)} %back_body.1.refs_2_, bf16[288,512]{1,0:T(8,128)(2,1)S(1)} %collective-permute-done.22.refs_3_, ...), custom_call_target="tpu_custom_call" | custom-call | bytes 3538944 | tf_op jit(solution)/shard_map/place_part/pallas_call | solution.py:480
  128.4 2.5 %collective-permute-done.21.refs_4_ = bf16[128,512]{1,0:T(8,128)(2,1)S(1)} collective-permute-done((bf16[128,512]{1,0:T(8,128)(2,1)S(1)}, bf16[128,512]{1,0:T(8,128)(2,1)S(1)}, u32[]{:S(2)}, u32[]{:S(2)}) %collective-permute-start.21) | collective-permute-done | bytes 131104 | tf_op jit(solution)/shard_map/ppermute | solution.py:503
  132.1 1.3 collective-permute-done.26.refs_5_
  133.5 1.4 %place_part.3 = bf16[1152,1024]{1,0:T(8,128)(2,1)} custom-call(s32[3]{0:T(128)S(1)} %pad_add_fusion.pos.spare.refs_0_, s32[88]{0:T(128)S(1)} %get-tuple-element.84.tab.refs_1_, bf16[160,512]{1,0:T(8,128)(2,1)S(1)} %collective-permute-done.20.refs_2_, bf16[160,512]{1,0:T(8,128)(2,1)S(1)} %collective-permute-done.25.refs_3_, ...), custom_call_target="tpu_custom_call", output_to_operand_aliasing={{}: (6, {})} | custom-call | bytes 1179648 | tf_op jit(solution)/shard_map/place_part/pallas_call | solution.py:480
  (72 shorter events, 11.5 us)
Async XLA Ops:
  0.6 7.7 %collective-permute-start = (bf16[1152,1024]{1,0:T(8,128)(2,1)}, bf16[1152,1024]{1,0:T(8,128)(2,1)S(1)}, u32[]{:S(2)}, u32[]{:S(2)}) collective-permute-start(bf16[1152,1024]{1,0:T(8,128)(2,1)} %bitcast.16), channel_id=1, source_target_pairs={{0,32},{32,0},{1,33},{33,1},{2,34},{34,2},{3,35},{35,3},{4,36},{36... | collective-permute-start | bytes 7077896 | tf_op jit(solution)/shard_map/ppermute | solution.py:507
  4.0 4.4 %collective-permute-start.1 = (bf16[1,1,1024]{2,1,0:T(2,128)(2,1)}, bf16[1,1,1024]{2,1,0:T(2,128)(2,1)S(1)}, u32[]{:S(2)}, u32[]{:S(2)}) collective-permute-start(bf16[1,1,1024]{2,1,0:T(2,128)(2,1)} %vec.1), channel_id=1, source_target_pairs={{0,32},{32,0},{1,33},{33,1},{2,34},{34,2},{3,35},{35,3},{4,36},{36... | collective-permute-start | bytes 6152 | tf_op jit(solution)/shard_map/ppermute | solution.py:507
  9.4 9.0 %collective-permute-start.2 = (bf16[320,512]{1,0:T(8,128)(2,1)S(1)}, bf16[320,512]{1,0:T(8,128)(2,1)S(1)}, u32[]{:S(2)}, u32[]{:S(2)}) collective-permute-start(bf16[320,512]{1,0:T(8,128)(2,1)S(1)} %get-tuple-element.88), channel_id=1, source_target_pairs={{0,64},{64,0},{128,192},{192,128},{1,65},{65,1},{129,193},{193,129... | collective-permute-start | bytes 983048 | tf_op jit(solution)/shard_map/ppermute | solution.py:503
  9.5 10.0 %collective-permute-start.4 = (bf16[288,512]{1,0:T(8,128)(2,1)S(1)}, bf16[288,512]{1,0:T(8,128)(2,1)S(1)}, u32[]{:S(2)}, u32[]{:S(2)}) collective-permute-start(bf16[288,512]{1,0:T(8,128)(2,1)S(1)} %get-tuple-element.90), channel_id=1, source_target_pairs={{0,192},{64,128},{128,64},{192,0},{1,193},{65,129},{129,65},{193,1... | collective-permute-start | bytes 884744 | tf_op jit(solution)/shard_map/ppermute | solution.py:503
  18.4 5.8 %collective-permute-start.3 = (bf16[160,512]{1,0:T(8,128)(2,1)S(1)}, bf16[160,512]{1,0:T(8,128)(2,1)S(1)}, u32[]{:S(2)}, u32[]{:S(2)}) collective-permute-start(bf16[160,512]{1,0:T(8,128)(2,1)S(1)} %slice_add_fusion), channel_id=1, source_target_pairs={{0,192},{64,128},{128,64},{192,0},{1,193},{65,129},{129,65},{193,1... | collective-permute-start | bytes 491528 | tf_op jit(solution)/shard_map/ppermute | solution.py:503
  19.5 4.1 %collective-permute-start.5 = (bf16[144,512]{1,0:T(8,128)(2,1)S(1)}, bf16[144,512]{1,0:T(8,128)(2,1)S(1)}, u32[]{:S(2)}, u32[]{:S(2)}) collective-permute-start(bf16[144,512]{1,0:T(8,128)(2,1)S(1)} %slice_add_fusion.1), channel_id=1, source_target_pairs={{0,64},{64,0},{128,192},{192,128},{1,65},{65,1},{129,193},{193,129... | collective-permute-start | bytes 442376 | tf_op jit(solution)/shard_map/ppermute | solution.py:503
  25.9 34.9 %all-to-all-start = ((bf16[32,32,512]{2,1,0:T(8,128)(2,1)}), bf16[32,32,512]{2,1,0:T(8,128)(2,1)S(1)}, u32[]{:S(2)}, u32[]{:S(2)}) async-start(bf16[32,32,512]{2,1,0:T(8,128)(2,1)} %bitcast.18), calls=%async_computation | async-start | bytes 2097152 | tf_op jit(solution)/shard_map/all_to_all | solution.py:512
  36.6 32.4 %copy-start.9 = (bf16[2048,128]{1,0:T(8,128)(2,1)S(1)}, bf16[2048,128]{1,0:T(8,128)(2,1)}, u32[]{:S(2)}) copy-start(bf16[2048,128]{1,0:T(8,128)(2,1)} %get-tuple-element.121.r0.refs_0_) | copy-start | bytes 1572868
  36.7 11.1 %collective-permute-start.6 = (bf16[2048,128]{1,0:T(8,128)(2,1)}, bf16[2048,128]{1,0:T(8,128)(2,1)S(1)}, u32[]{:S(2)}, u32[]{:S(2)}) collective-permute-start(bf16[2048,128]{1,0:T(8,128)(2,1)} %get-tuple-element.107), channel_id=1, source_target_pairs={{0,64},{64,0},{128,192},{192,128},{1,65},{65,1},{129,193},{193,129... | collective-permute-start | bytes 1572872 | tf_op jit(solution)/shard_map/ppermute | solution.py:503
  36.8 12.3 %collective-permute-start.7 = (bf16[2048,128]{1,0:T(8,128)(2,1)}, bf16[2048,128]{1,0:T(8,128)(2,1)S(1)}, u32[]{:S(2)}, u32[]{:S(2)}) collective-permute-start(bf16[2048,128]{1,0:T(8,128)(2,1)} %get-tuple-element.108), channel_id=1, source_target_pairs={{0,192},{64,128},{128,64},{192,0},{1,193},{65,129},{129,65},{193,1... | collective-permute-start | bytes 1572872 | tf_op jit(solution)/shard_map/ppermute | solution.py:503
  38.1 22.1 %collective-permute-start.8 = (bf16[2048,128]{1,0:T(8,128)(2,1)}, bf16[2048,128]{1,0:T(8,128)(2,1)S(1)}, u32[]{:S(2)}, u32[]{:S(2)}) collective-permute-start(bf16[2048,128]{1,0:T(8,128)(2,1)} %get-tuple-element.109), channel_id=1, source_target_pairs={{0,128},{64,192},{128,0},{192,64},{1,129},{65,193},{129,1},{193,65... | collective-permute-start | bytes 1572872 | tf_op jit(solution)/shard_map/ppermute | solution.py:503
  40.0 4.3 %collective-permute-start.9 = (bf16[16,128]{1,0:T(8,128)(2,1)S(1)}, bf16[16,128]{1,0:T(8,128)(2,1)S(1)}, u32[]{:S(2)}, u32[]{:S(2)}) collective-permute-start(bf16[16,128]{1,0:T(8,128)(2,1)S(1)} %get-tuple-element.110.step), channel_id=1, source_target_pairs={{0,32},{32,0},{1,33},{33,1},{2,34},{34,2},{3,35},{35,3},{4,36},{36... | collective-permute-start | bytes 12296 | tf_op jit(solution)/shard_map/ppermute | solution.py:507
  47.8 18.5 %copy-start.10 = (bf16[2048,128]{1,0:T(8,128)(2,1)}, bf16[2048,128]{1,0:T(8,128)(2,1)S(1)}, u32[]{:S(2)}) copy-start(bf16[2048,128]{1,0:T(8,128)(2,1)S(1)} %collective-permute-done.6.r1.refs_1_) | copy-start | bytes 1572868
  60.8 8.2 %collective-permute-start.10 = (bf16[1024,512]{1,0:T(8,128)(2,1)S(1)}, bf16[1024,512]{1,0:T(8,128)(2,1)S(1)}, u32[]{:S(2)}, u32[]{:S(2)}) collective-permute-start(bf16[1024,512]{1,0:T(8,128)(2,1)S(1)} %bitcast.9), channel_id=1, source_target_pairs={{0,32},{32,0},{1,33},{33,1},{2,34},{34,2},{3,35},{35,3},{4,36},{36... | collective-permute-start | bytes 3145736 | tf_op jit(solution)/shard_map/ppermute | solution.py:507
  69.1 4.3 %collective-permute-start.11 = (bf16[2048,128]{1,0:T(8,128)(2,1)S(1)}, bf16[2048,128]{1,0:T(8,128)(2,1)S(1)}, u32[]{:S(2)}, u32[]{:S(2)}) collective-permute-start(bf16[2048,128]{1,0:T(8,128)(2,1)S(1)} %copy-done.9), channel_id=1, source_target_pairs={{0,32},{32,0},{1,33},{33,1},{2,34},{34,2},{3,35},{35,3},{4,36},{36... | collective-permute-start | bytes 1572872 | tf_op jit(solution)/shard_map/ppermute | solution.py:507
  69.2 4.2 %collective-permute-start.12 = (bf16[2048,128]{1,0:T(8,128)(2,1)}, bf16[2048,128]{1,0:T(8,128)(2,1)S(1)}, u32[]{:S(2)}, u32[]{:S(2)}) collective-permute-start(bf16[2048,128]{1,0:T(8,128)(2,1)} %copy-done.10), channel_id=1, source_target_pairs={{0,32},{32,0},{1,33},{33,1},{2,34},{34,2},{3,35},{35,3},{4,36},{36... | collective-permute-start | bytes 1572872 | tf_op jit(solution)/shard_map/ppermute | solution.py:507
  69.7 3.7 %collective-permute-start.13 = (bf16[2048,128]{1,0:T(8,128)(2,1)}, bf16[2048,128]{1,0:T(8,128)(2,1)S(1)}, u32[]{:S(2)}, u32[]{:S(2)}) collective-permute-start(bf16[2048,128]{1,0:T(8,128)(2,1)} %copy-done.12), channel_id=1, source_target_pairs={{0,32},{32,0},{1,33},{33,1},{2,34},{34,2},{3,35},{35,3},{4,36},{36... | collective-permute-start | bytes 1572872 | tf_op jit(solution)/shard_map/ppermute | solution.py:507
  69.8 3.8 %collective-permute-start.14 = (bf16[2048,128]{1,0:T(8,128)(2,1)}, bf16[2048,128]{1,0:T(8,128)(2,1)S(1)}, u32[]{:S(2)}, u32[]{:S(2)}) collective-permute-start(bf16[2048,128]{1,0:T(8,128)(2,1)} %copy-done.11), channel_id=1, source_target_pairs={{0,32},{32,0},{1,33},{33,1},{2,34},{34,2},{3,35},{35,3},{4,36},{36... | collective-permute-start | bytes 1572872 | tf_op jit(solution)/shard_map/ppermute | solution.py:507
  77.8 33.3 %all-to-all-start.1 = ((bf16[32,32,512]{2,1,0:T(8,128)(2,1)}), bf16[32,32,512]{2,1,0:T(8,128)(2,1)S(1)}, u32[]{:S(2)}, u32[]{:S(2)}) async-start(bf16[32,32,512]{2,1,0:T(8,128)(2,1)} %bitcast.15), calls=%async_computation.1 | async-start | bytes 2097152 | tf_op jit(solution)/shard_map/all_to_all | solution.py:512
  85.3 13.3 %collective-permute-start.15 = (bf16[2080,128]{1,0:T(8,128)(2,1)}, bf16[2080,128]{1,0:T(8,128)(2,1)S(1)}, u32[]{:S(2)}, u32[]{:S(2)}) collective-permute-start(bf16[2080,128]{1,0:T(8,128)(2,1)} %get-tuple-element.141), channel_id=1, source_target_pairs={{0,64},{64,0},{128,192},{192,128},{1,65},{65,1},{129,193},{193,129... | collective-permute-start | bytes 1597448 | tf_op jit(solution)/shard_map/ppermute | solution.py:503
  85.6 14.1 %collective-permute-start.16 = (bf16[2080,128]{1,0:T(8,128)(2,1)}, bf16[2080,128]{1,0:T(8,128)(2,1)S(1)}, u32[]{:S(2)}, u32[]{:S(2)}) collective-permute-start(bf16[2080,128]{1,0:T(8,128)(2,1)} %get-tuple-element.142), channel_id=1, source_target_pairs={{0,192},{64,128},{128,64},{192,0},{1,193},{65,129},{129,65},{193,1... | collective-permute-start | bytes 1597448 | tf_op jit(solution)/shard_map/ppermute | solution.py:503
  86.9 24.2 %collective-permute-start.17 = (bf16[2080,128]{1,0:T(8,128)(2,1)S(1)}, bf16[2080,128]{1,0:T(8,128)(2,1)S(1)}, u32[]{:S(2)}, u32[]{:S(2)}) collective-permute-start(bf16[2080,128]{1,0:T(8,128)(2,1)S(1)} %copy-done.13), channel_id=1, source_target_pairs={{0,128},{64,192},{128,0},{192,64},{1,129},{65,193},{129,1},{193,65... | collective-permute-start | bytes 1597448 | tf_op jit(solution)/shard_map/ppermute | solution.py:503
  98.6 18.5 %copy-start.6 = (bf16[2080,128]{1,0:T(8,128)(2,1)}, bf16[2080,128]{1,0:T(8,128)(2,1)S(1)}, u32[]{:S(2)}) copy-start(bf16[2080,128]{1,0:T(8,128)(2,1)S(1)} %collective-permute-done.15.g1) | copy-start | bytes 1597444
  111.7 10.8 %collective-permute-start.18 = (bf16[288,512]{1,0:T(8,128)(2,1)S(1)}, bf16[288,512]{1,0:T(8,128)(2,1)S(1)}, u32[]{:S(2)}, u32[]{:S(2)}) collective-permute-start(bf16[288,512]{1,0:T(8,128)(2,1)S(1)} %back_body.1.refs_2_), channel_id=1, source_target_pairs={{0,192},{64,128},{128,64},{192,0},{1,193},{65,129},{129,65},{193,1... | collective-permute-start | bytes 884744 | tf_op jit(solution)/shard_map/ppermute | solution.py:503
  113.2 9.4 %collective-permute-start.19 = (bf16[288,512]{1,0:T(8,128)(2,1)S(1)}, bf16[288,512]{1,0:T(8,128)(2,1)S(1)}, u32[]{:S(2)}, u32[]{:S(2)}) collective-permute-start(bf16[288,512]{1,0:T(8,128)(2,1)S(1)} %back_body.1.refs_2_), channel_id=1, source_target_pairs={{0,64},{64,0},{128,192},{192,128},{1,65},{65,1},{129,193},{193,129... | collective-permute-start | bytes 884744 | tf_op jit(solution)/shard_map/ppermute | solution.py:503
  113.2 13.2 %collective-permute-start.22 = (bf16[288,512]{1,0:T(8,128)(2,1)S(1)}, bf16[288,512]{1,0:T(8,128)(2,1)S(1)}, u32[]{:S(2)}, u32[]{:S(2)}) collective-permute-start(bf16[288,512]{1,0:T(8,128)(2,1)S(1)} %back_body.1.refs_2_), channel_id=1, source_target_pairs={{0,32},{32,0},{1,33},{33,1},{2,34},{34,2},{3,35},{35,3},{4,36},{36... | collective-permute-start | bytes 884744 | tf_op jit(solution)/shard_map/ppermute | solution.py:507
  122.5 3.9 %collective-permute-start.23 = (bf16[288,512]{1,0:T(8,128)(2,1)S(1)}, bf16[288,512]{1,0:T(8,128)(2,1)S(1)}, u32[]{:S(2)}, u32[]{:S(2)}) collective-permute-start(bf16[288,512]{1,0:T(8,128)(2,1)S(1)} %collective-permute-done.18.refs_4_), channel_id=1, source_target_pairs={{0,32},{32,0},{1,33},{33,1},{2,34},{34,2},{3,35},{35,3},{4,36},{36... | collective-permute-start | bytes 884744 | tf_op jit(solution)/shard_map/ppermute | solution.py:507
  123.9 2.5 %collective-permute-start.24 = (bf16[288,512]{1,0:T(8,128)(2,1)S(1)}, bf16[288,512]{1,0:T(8,128)(2,1)S(1)}, u32[]{:S(2)}, u32[]{:S(2)}) collective-permute-start(bf16[288,512]{1,0:T(8,128)(2,1)S(1)} %collective-permute-done.19.refs_6_), channel_id=1, source_target_pairs={{0,32},{32,0},{1,33},{33,1},{2,34},{34,2},{3,35},{35,3},{4,36},{36... | collective-permute-start | bytes 884744 | tf_op jit(solution)/shard_map/ppermute | solution.py:507
  123.9 7.0 %collective-permute-start.20 = (bf16[160,512]{1,0:T(8,128)(2,1)S(1)}, bf16[160,512]{1,0:T(8,128)(2,1)S(1)}, u32[]{:S(2)}, u32[]{:S(2)}) collective-permute-start(bf16[160,512]{1,0:T(8,128)(2,1)S(1)} %slice.26), channel_id=1, source_target_pairs={{0,64},{64,0},{128,192},{192,128},{1,65},{65,1},{129,193},{193,129... | collective-permute-start | bytes 491528 | tf_op jit(solution)/shard_map/ppermute | solution.py:503
  124.9 6.0 %collective-permute-start.21 = (bf16[128,512]{1,0:T(8,128)(2,1)S(1)}, bf16[128,512]{1,0:T(8,128)(2,1)S(1)}, u32[]{:S(2)}, u32[]{:S(2)}) collective-permute-start(bf16[128,512]{1,0:T(8,128)(2,1)S(1)} %slice.27), channel_id=1, source_target_pairs={{0,192},{64,128},{128,64},{192,0},{1,193},{65,129},{129,65},{193,1... | collective-permute-start | bytes 393224 | tf_op jit(solution)/shard_map/ppermute | solution.py:503
  130.9 2.5 %collective-permute-start.25 = (bf16[160,512]{1,0:T(8,128)(2,1)S(1)}, bf16[160,512]{1,0:T(8,128)(2,1)S(1)}, u32[]{:S(2)}, u32[]{:S(2)}) collective-permute-start(bf16[160,512]{1,0:T(8,128)(2,1)S(1)} %collective-permute-done.20.refs_2_), channel_id=1, source_target_pairs={{0,32},{32,0},{1,33},{33,1},{2,34},{34,2},{3,35},{35,3},{4,36},{36... | collective-permute-start | bytes 491528 | tf_op jit(solution)/shard_map/ppermute | solution.py:507
  132.1 1.3 collective-permute-start.26
  (11 other events, 137.9 us)
